TPU v7x, 32 devices: a whole 2x2x4 slice. The times are simulated.
32 devices in a mesh: pipe: 2 (over y), ctx: 8 (over z, x), tp: 2 (over core).
Axes of the slice: x: 2, y: 2, z: 4, core: 2. Of those that a mesh axis runs over, the one named last changes fastest.
Arguments:
- stream: bfloat16 [2, 1024, 4096], P('pipe', 'ctx', 'tp'), may hold values from -6 to 6
- queries: bfloat16 [2, 1024, 4096], P('pipe', 'ctx', 'tp'), may hold values from -5 to 5
- keys: bfloat16 [2, 1024, 1024], P('pipe', 'ctx', 'tp'), may hold values from -5 to 5
- values: bfloat16 [2, 1024, 1024], P('pipe', 'ctx', 'tp'), may hold values from -6 to 6
- segments: int32 [2, 1024], P('pipe', 'ctx'), may hold values from 0 to 5, never falling along the last dimension, each value on 1 to 512 neighbouring positions
- norm_gain: bfloat16 [4096], P('tp'), may hold values from 0.25 to 1.75
Outputs:
- arrived: bfloat16 [2, 1024, 4096], P('pipe', 'ctx', 'tp')
- normed: bfloat16 [2, 1024, 4096], P('pipe', 'ctx', 'tp')
Inputs may be any that keep to these rules, and one draw needn't show every extreme that they name: `segments`: in each section's micro-batch the document number never falls along positions; each document holds 1 to half of 1024 positions, and one holds exactly half of 1024.
All inputs are finite; a program needn't handle non-finite values.
Results may differ from a plain program's by a relative error of at most 0.006.
Values may be sent and summed in bfloat16 or wider, within the bound.
No kernel may reach another device: no remote copies, remote signals or barrier semaphores. Data moves between devices by JAX's collectives and lax.ppermute only.
A program may use at most 128 MiB of HBM per device.

v0:
```python
import jax
import jax.numpy as jnp
from jax import lax
from jax.sharding import PartitionSpec as P

QUERY_HEADS = 32
HEAD_SIZE = 128


def from_behind(block, axis, distance):
    devices = range(lax.axis_size(axis))
    route = [((i - distance) % len(devices), i) for i in devices]
    return lax.ppermute(block, axis, route)


def per_device(stream, queries, keys, values, segments, norm_gain):
    row_count = stream.shape[1]
    kv_width = keys.shape[2]
    kv_heads = kv_width // HEAD_SIZE
    query_group_size = queries.shape[2] // kv_width
    score_scale = HEAD_SIZE ** (-0.5)
    ctx_index = lax.axis_index("ctx")
    query_head_stack = (
        queries[0]
        .reshape(row_count, kv_heads, query_group_size, HEAD_SIZE)
        .transpose(1, 2, 0, 3)
        .reshape(kv_heads, query_group_size * row_count, HEAD_SIZE)
    )
    own_pos = ctx_index * row_count + jnp.arange(row_count, dtype=jnp.int32)
    query_pos = jnp.tile(own_pos, query_group_size)
    query_seg = jnp.tile(segments[0], query_group_size)
    query_row_block = query_group_size * row_count
    key_piece = lax.all_gather(keys[0], "ctx", axis=0, tiled=True)
    running_max = jnp.full((kv_heads, query_row_block), -1e30, jnp.float32)
    key_count = key_piece.shape[0]
    key_head_stack = key_piece.reshape(key_count, kv_heads, HEAD_SIZE)
    value_head_stack = lax.all_gather(values[0], "ctx", axis=0, tiled=True).reshape(
        key_count, kv_heads, HEAD_SIZE
    )
    scores = (
        jnp.einsum(
            "hrd,khd->hrk", query_head_stack, key_head_stack, preferred_element_type=jnp.float32
        )
        * score_scale
    )
    key_pos = jnp.arange(key_count, dtype=jnp.int32)
    allowed = (
        (key_pos[None, :] <= query_pos[:, None])
        & (lax.all_gather(segments[0], "ctx", axis=0, tiled=True)[None, :] == query_seg[:, None])
        & jnp.bool_(True)
    )
    scores = jnp.where(allowed[None], scores, -1e30)
    new_max = jnp.maximum(running_max, jnp.max(scores, axis=-1))
    weights = jnp.where(allowed[None], jnp.exp(scores - new_max[..., None]), 0.0)
    new_sum = jnp.sum(weights, axis=-1)
    new_acc = jnp.einsum(
        "hrk,khd->hrd",
        weights.astype(jnp.bfloat16),
        value_head_stack,
        preferred_element_type=jnp.float32,
    )
    final_state = (new_max, new_sum, new_acc)
    running_max, running_sum, running_acc = final_state
    mixed = (running_acc / running_sum[..., None]).astype(jnp.bfloat16)
    attended = (
        mixed.reshape(kv_heads, query_group_size, row_count, HEAD_SIZE)
        .transpose(2, 0, 1, 3)
        .reshape(row_count, kv_width * query_group_size)
    )
    attended = lax.optimization_barrier(attended).astype(jnp.float32)
    advanced = (stream[0].astype(jnp.float32) + attended).astype(jnp.bfloat16)
    arrived = from_behind(advanced[None], "pipe", 1)
    wide = arrived.astype(jnp.float32)
    squares = jnp.sum(wide * wide, axis=-1)
    totals = lax.psum(squares, "tp")
    inverse = lax.rsqrt(totals / (QUERY_HEADS * HEAD_SIZE) + 1e-05)
    normed = (wide * inverse[..., None] * norm_gain.astype(jnp.float32)).astype(jnp.bfloat16)
    return (arrived, normed)


def solution(mesh):
    in_specs = (
        P("pipe", "ctx", "tp"),
        P("pipe", "ctx", "tp"),
        P("pipe", "ctx", "tp"),
        P("pipe", "ctx", "tp"),
        P("pipe", "ctx"),
        P("tp"),
    )
    out_specs = (P("pipe", "ctx", "tp"), P("pipe", "ctx", "tp"))
    return jax.shard_map(
        per_device, mesh=mesh, in_specs=in_specs, out_specs=out_specs, check_vma=False
    )
```

profile of v0, /device:TPU:1, one launch (start us, length us, event | category | flops | bytes accessed | tf_op | source)
XLA Modules:
  0.0 125.1 jit_solution(1048477385171096715)
XLA Ops:
  7.2 0.0 all-gather.6.cloned.1.call-start
  7.2 1.7 %copy.11 = bf16[1,128,512]{1,2,0:T(8,128)(2,1)} copy(bf16[1,128,512]{2,1,0:T(8,128)(2,1)} %param.8) | data formatting | bytes 262144 | tf_op args[2]
  8.9 0.0 all-gather.6.cloned.1.call-update
  8.9 0.0 all-gather.8.cloned.1.call-start
  8.9 1.7 %copy.13 = bf16[1,128,512]{1,2,0:T(8,128)(2,1)} copy(bf16[1,128,512]{2,1,0:T(8,128)(2,1)} %param.9) | data formatting | bytes 262144 | tf_op args[3]
  10.6 0.0 all-gather.8.cloned.1.call-update
  10.7 17.9 %all-gather = s32[1,1024]{1,0:T(1,128)S(1)} all-gather(s32[1,128]{1,0:T(1,128)} %param.10), channel_id=2, replica_groups=mesh['pipe'=2,'ctx'=8,'tp'=2] {'ctx'}, dimensions={1}, use_global_device_ids=true | all-gather | bytes 4608 | tf_op jit(solution)/shard_map/all_gather | solution.py:49
  28.6 1.4 %reshape_squeeze.3 = bf16[128,4,4,128]{3,2,1,0:T(4,128)(2,1)S(1)} reshape(bf16[1,128,2048]{2,1,0:T(8,128)(2,1)} %param.7) | data formatting | bytes 1048576 | tf_op jit(solution)/shard_map/reshape;squeeze | solution.py:25
  30.0 0.1 copy.10
  30.1 0.7 broadcast_bitcast_fusion
  30.8 0.5 fusion.6
  31.3 18.6 %all-gather.6.cloned.1.call-done = bf16[1,1024,512]{1,2,0:T(8,128)(2,1)} async-done(((bf16[1,128,512]{1,2,0:T(8,128)(2,1)}), bf16[1,1024,512]{1,2,0:T(8,128)(2,1)}) %all-gather.6.cloned.1.call-update) | async-done | bytes 1048592 | tf_op jit(solution)/shard_map/all_gather | solution.py:33
  49.9 3.1 %fusion = (f32[4,512]{1,0:T(4,128)S(1)}, f32[4,512,1024]{2,1,0:T(8,128)S(1)}) fusion(pred[512,1024]{1,0:T(8,128)(4,1)S(1)} %fusion.6, bf16[4,512,128]{2,1,0:T(8,128)(2,1)S(1)} %bitcast.24, bf16[1024,4,128]{0,2,1:T(8,128)(2,1)} %bitcast.26), kind=kOutput, calls=%fused_computation.2 | convolution fusion | flops 543160320 | bytes 10493952 | tf_op jit(solution)/shard_map/hrd,khd->hrk/dot_general | solution.py:41
  53.0 0.0 copy-start
  53.0 3.2 %copy-done = f32[4,512,1024]{2,1,0:T(8,128)} copy-done((f32[4,512,1024]{2,1,0:T(8,128)}, f32[4,512,1024]{2,1,0:T(8,128)S(1)}, u32[]{:S(2)}) %copy-start) | copy-done | bytes 8388632
  56.2 3.0 %fusion.1 = f32[4,512]{1,0:T(4,128)S(1)} fusion(f32[4,512,1024]{2,1,0:T(8,128)S(1)} %get-tuple-element.3, f32[4,512]{1,0:T(4,128)S(1)} %broadcast_maximum_fusion, pred[512,1024]{1,0:T(8,128)(4,1)S(1)} %fusion.6), kind=kLoop, calls=%fused_computation.3 | loop fusion | flops 10483712 | bytes 8929280 | tf_op jit(solution)/shard_map/reduce_sum | solution.py:55
  59.2 31.8 %all-gather.8.cloned.1.call-done = bf16[1,1024,512]{1,2,0:T(8,128)(2,1)} async-done(((bf16[1,128,512]{1,2,0:T(8,128)(2,1)}), bf16[1,1024,512]{1,2,0:T(8,128)(2,1)}) %all-gather.8.cloned.1.call-update) | async-done | bytes 1048592 | tf_op jit(solution)/shard_map/all_gather | solution.py:37
  91.0 0.0 copy-start.1
  91.0 0.0 copy-start.2
  91.0 6.0 %divide_convert_fusion = bf16[4,512,128]{2,1,0:T(8,128)(2,1)S(1)} fusion(bf16[1024,4,128]{0,2,1:T(8,128)(2,1)} %bitcast.31, f32[4,512,1024]{2,1,0:T(8,128)} %copy-done, f32[4,512]{1,0:T(4,128)S(1)} %broadcast_maximum_fusion, pred[512,1024]{1,0:T(8,128)(4,1)S(1)} %fusion.6, f32[4,512]{1,0:T(4,128)S(1)} %fusion.1), kind=kOutput, calls=%fused_computation.16 | convolution fusion | flops 547880960 | bytes 10502144 | tf_op jit(solution)/shard_map/hrk,khd->hrd/dot_general | solution.py:56
  97.0 0.4 copy.15
  97.4 0.4 reshape.92
  97.8 0.0 copy-done.1
  97.8 0.1 fusion.13
  97.9 3.3 %collective-permute-start = (bf16[1,128,2048]{2,1,0:T(8,128)(2,1)S(1)}, bf16[1,128,2048]{2,1,0:T(8,128)(2,1)S(1)}, u32[]{:S(2)}, u32[]{:S(2)}) collective-permute-start(bf16[1,128,2048]{2,1,0:T(8,128)(2,1)S(1)} %fusion.13), channel_id=1, source_target_pairs={{16,0},{0,16},{17,1},{1,17},{18,2},{2,18},{19,3},{3,19},{20,4},{4,... | collective-permute-start | bytes 1572872 | tf_op jit(solution)/shard_map/ppermute | solution.py:13
  101.3 0.0 copy-done.2
  101.3 10.7 %collective-permute-done = bf16[1,128,2048]{2,1,0:T(8,128)(2,1)S(1)} collective-permute-done((bf16[1,128,2048]{2,1,0:T(8,128)(2,1)S(1)}, bf16[1,128,2048]{2,1,0:T(8,128)(2,1)S(1)}, u32[]{:S(2)}, u32[]{:S(2)}) %collective-permute-start) | collective-permute-done | bytes 524320 | tf_op jit(solution)/shard_map/ppermute | solution.py:13
  111.9 0.2 fusion.7
  112.1 4.3 %psum.7 = f32[1,128]{1,0:T(1,128)S(1)} all-reduce(f32[1,128]{1,0:T(1,128)S(1)} %bitcast.30), channel_id=1, replica_groups=mesh['pipe'=2,'ctx'=8,'tp'=2] {'tp'}, use_global_device_ids=true, to_apply=%region_3.4 | all-reduce | flops 128 | bytes 1024 | tf_op jit(solution)/shard_map/psum | solution.py:75
  116.5 1.0 fusion.9
  117.4 0.8 copy.19
  (4 shorter events, 0.0 us)
Async XLA Ops:
  7.2 42.7 %all-gather.6.cloned.1.call-start = ((), (), s32[]{:S(2)}) async-start(), calls=%async_computation | async-start | bytes 1179648 | tf_op jit(solution)/shard_map/all_gather | solution.py:33
  8.9 82.1 %all-gather.8.cloned.1.call-start = ((), (), s32[]{:S(2)}) async-start(), calls=%async_computation.1 | async-start | bytes 1179648 | tf_op jit(solution)/shard_map/all_gather | solution.py:37
  53.0 3.2 %copy-start = (f32[4,512,1024]{2,1,0:T(8,128)}, f32[4,512,1024]{2,1,0:T(8,128)S(1)}, u32[]{:S(2)}) copy-start(f32[4,512,1024]{2,1,0:T(8,128)S(1)} %get-tuple-element.3) | copy-start | bytes 25165828
  91.0 6.8 %copy-start.1 = (bf16[1,128,2048]{2,1,0:T(8,128)(2,1)S(1)}, bf16[1,128,2048]{2,1,0:T(8,128)(2,1)}, u32[]{:S(2)}) copy-start(bf16[1,128,2048]{2,1,0:T(8,128)(2,1)} %param.6) | copy-start | bytes 1572868
  91.0 10.3 %copy-start.2 = (bf16[2048]{0:T(1024)(128)(2,1)S(1)}, bf16[2048]{0:T(1024)(128)(2,1)}, u32[]{:S(2)}) copy-start(bf16[2048]{0:T(1024)(128)(2,1)} %param.11) | copy-start | bytes 12292
  97.9 14.0 %collective-permute-start = (bf16[1,128,2048]{2,1,0:T(8,128)(2,1)S(1)}, bf16[1,128,2048]{2,1,0:T(8,128)(2,1)S(1)}, u32[]{:S(2)}, u32[]{:S(2)}) collective-permute-start(bf16[1,128,2048]{2,1,0:T(8,128)(2,1)S(1)} %fusion.13), channel_id=1, source_target_pairs={{16,0},{0,16},{17,1},{1,17},{18,2},{2,18},{19,3},{3,19},{20,4},{4,... | collective-permute-start | bytes 1572872 | tf_op jit(solution)/shard_map/ppermute | solution.py:13
Sparse Core Ops, SparseCore 0:
  10.6 39.2 all-gather.5
  52.5 38.4 all-gather.7
where the time goes:
time: 126 us; the launch traced here: 125 us
  waiting for transfers between devices  61.1 us (48%)
  blocking collectives  22.3 us (18%)
  between operations  14.1 us (11%)
  local copies, waits for them, and re-layouts  10.3 us (8%)
  matrix products  9.04 us (7%)
  other arithmetic  4.85 us (4%)
  starting transfers between devices  3.42 us (3%)
    all_gather x1, waiting for transfers between devices, per_device(): lax.all_gather(values[0], 'ctx', axis=0, tiled=True)  31.8 us
    all_gather x1, waiting for transfers between devices, per_device(): key_piece = lax.all_gather(keys[0], 'ctx', axis=0, tiled=True)  18.6 us
    all_gather x1, blocking collectives, per_device(): lax.all_gather(segments[0], 'ctx', axis=0, tiled=True)[None, :]  17.9 us
    ppermute x1, waiting for transfers between devices, from_behind(): return lax.ppermute(block, axis, route)  10.7 us
    unnamed x9, local copies, waits for them, and re-layouts  7.33 us
    dot_general x1, matrix products, per_device(): jnp.einsum('hrk,khd->hrd', weights.astype(jnp.bfloat16), value_head_stack...  5.97 us
    psum x1, blocking collectives, per_device(): totals = lax.psum(squares, 'tp')  4.33 us
    ppermute x1, starting transfers between devices, from_behind(): return lax.ppermute(block, axis, route)  3.34 us
  transfers between devices with their start and end apart: 3, of which 3 were waited for; matrix products, arithmetic and copies ran while one was open for 8% of the time, Pallas kernels for 0%

commit v1 on v0

v1 whole, which is shorter than its diff:
```python
import functools
import math

import jax
import jax.numpy as jnp
from jax import lax
from jax.experimental import pallas as pl
from jax.experimental.pallas import tpu as pltpu
from jax.sharding import PartitionSpec as P

HEAD = 128
FEATURES = 4096
EPS = 1e-05
SEG_ROWS = 16
NEG = -1e30
VMEM_LIMIT = 40 * 1024 * 1024


def route(x, axes, move):
    sizes = [lax.axis_size(a) for a in axes]
    pairs = []
    for src in range(math.prod(sizes)):
        at, rest = [], src
        for s in reversed(sizes):
            at.insert(0, rest % s)
            rest //= s
        to = 0
        for s, v in zip(sizes, move(*at)):
            to = to * s + v
        pairs.append((src, to))
    return lax.ppermute(x, tuple(axes) if len(axes) > 1 else axes[0], pairs)


def turned(row):
    return jnp.transpose(jnp.broadcast_to(row, (HEAD, HEAD)))


def pack_kernel(halves, k_ref, v_ref, seg_ref, keep_ref, send_ref):
    side = lax.axis_index("ctx") % 2
    seg = jnp.broadcast_to(seg_ref[...], (SEG_ROWS, HEAD)).astype(jnp.float32).astype(jnp.bfloat16)
    for out, half in ((keep_ref, side), (send_ref, 1 - side)):
        for h in range(halves):
            at = pl.ds(pl.multiple_of((half * halves + h) * HEAD, HEAD), HEAD)
            out[2 * h * HEAD : (2 * h + 1) * HEAD, :] = k_ref[0, :, at]
            out[(2 * h + 1) * HEAD : (2 * h + 2) * HEAD, :] = v_ref[0, :, at]
        out[2 * halves * HEAD :, :] = seg


def attend_kernel(stage, halves, group, levels_back, *refs):
    q_ref, s_ref, xq_ref, xs_ref = refs[:4]
    packs = refs[4 : 4 + 2 * (levels_back + 1)]
    own_out, part_out, own_sq, part_sq = refs[4 + 2 * (levels_back + 1) :]
    rows = HEAD
    width = group * HEAD
    ctx = lax.axis_index("ctx")
    side = ctx % 2
    seg_at = 2 * halves * HEAD
    own_pos, part_pos = ctx * rows, (ctx + 1 - 2 * side) * rows

    def seg_of(pack):
        return pack[seg_at : seg_at + SEG_ROWS, :].astype(jnp.float32)[:1]

    lane = lax.broadcasted_iota(jnp.int32, (rows, rows), 1)
    line = lax.broadcasted_iota(jnp.int32, (rows, rows), 0)
    bias = []
    for q_start, q_pack in ((own_pos, packs[0]), (part_pos, packs[1])):
        q_seg = turned(seg_of(q_pack))
        tiles = []
        for n, pack in enumerate(packs):
            k_start = (own_pos, part_pos)[n % 2] - (n // 2) * 2 * rows
            ok = (lane + k_start <= line + q_start) & (lane + k_start >= 0)
            ok &= q_seg == jnp.broadcast_to(seg_of(pack), (rows, rows))
            tiles.append(jnp.where(ok, 0.0, NEG))
        bias.append(jnp.concatenate(tiles, axis=1))
    bias = jnp.concatenate(bias, axis=0)
    at = 2 * stage * HEAD
    keys = jnp.concatenate([p[at : at + HEAD, :] for p in packs], axis=0)
    vals = jnp.concatenate([p[at + HEAD : at + 2 * HEAD, :] for p in packs], axis=0)
    scale = HEAD ** (-0.5) * math.log2(math.e)
    sq = [jnp.zeros((rows, HEAD), jnp.float32), jnp.zeros((rows, HEAD), jnp.float32)]
    for g in range(group):
        here = pl.ds(pl.multiple_of((side * halves + stage) * width + g * HEAD, HEAD), HEAD)
        there = slice(stage * width + g * HEAD, stage * width + (g + 1) * HEAD)
        q = jnp.concatenate([q_ref[0, :, here], xq_ref[:, there]], axis=0)
        s = lax.dot_general(q, keys, (((1,), (1,)), ((), ())), preferred_element_type=jnp.float32)
        s = s * scale + bias
        w = jnp.exp2(s - jnp.max(s, axis=1, keepdims=True))
        total = jnp.sum(w, axis=1, keepdims=True)
        att = jnp.dot(w.astype(jnp.bfloat16), vals, preferred_element_type=jnp.float32) / total
        att = att.astype(jnp.bfloat16).astype(jnp.float32)
        for n, (out, stream) in enumerate(
            ((own_out, s_ref[0, :, here]), (part_out, xs_ref[:, there]))
        ):
            adv = stream.astype(jnp.float32) + att[n * rows : (n + 1) * rows]
            adv = adv.astype(jnp.bfloat16)
            out[:, g * HEAD : (g + 1) * HEAD] = adv
            sq[n] += adv.astype(jnp.float32) ** 2
    for out, part in ((own_sq, sq[0]), (part_sq, sq[1])):
        out[...] = jnp.broadcast_to(jnp.sum(jnp.transpose(part), axis=0, keepdims=True), (8, HEAD))


def final_kernel(halves, width, *refs):
    own_parts, part_parts = refs[:halves], refs[halves : 2 * halves]
    sq_a, sq_b, gain_ref, arrived_ref, normed_ref = refs[2 * halves :]
    side = lax.axis_index("ctx") % 2
    sq = jnp.zeros((HEAD, HEAD), jnp.float32)
    for p in own_parts + part_parts:
        for g in range(width // HEAD):
            sq += p[:, g * HEAD : (g + 1) * HEAD].astype(jnp.float32) ** 2
    total = jnp.sum(jnp.transpose(sq), axis=0, keepdims=True) + sq_a[:1] + sq_b[:1]
    inv = turned(lax.rsqrt(total / FEATURES + EPS))
    for half, parts in ((side, own_parts), (1 - side, part_parts)):
        for n, p in enumerate(parts):
            for g in range(width // HEAD):
                at = pl.ds(pl.multiple_of((half * halves + n) * width + g * HEAD, HEAD), HEAD)
                a = p[:, g * HEAD : (g + 1) * HEAD]
                arrived_ref[0, :, at] = a
                gain = gain_ref[:, at].astype(jnp.float32)
                normed_ref[0, :, at] = (a.astype(jnp.float32) * inv * gain).astype(jnp.bfloat16)


def per_device(stream, queries, keys, values, segments, norm_gain):
    rows = stream.shape[1]
    kv_heads = keys.shape[2] // HEAD
    halves = kv_heads // 2
    group = queries.shape[2] // keys.shape[2]
    width = group * HEAD
    half_width = halves * width
    n_ctx = lax.axis_size("ctx")
    n_pipe = lax.axis_size("pipe")
    level = 2 * rows
    levels_back = (n_ctx * rows // 2 - 1 + level - 1) // level
    side = lax.axis_index("ctx") % 2
    pack_shape = (2 * halves * HEAD + SEG_ROWS, HEAD)
    vmem = pl.BlockSpec(memory_space=pltpu.VMEM)
    params = pltpu.CompilerParams(vmem_limit_bytes=VMEM_LIMIT)

    keep, send = pl.pallas_call(
        functools.partial(pack_kernel, halves),
        out_shape=[jax.ShapeDtypeStruct(pack_shape, jnp.bfloat16)] * 2,
        in_specs=[vmem] * 3,
        out_specs=[vmem] * 2,
        compiler_params=params,
        name="pack",
    )(keys, values, segments)

    def other(c):
        return (c + 1 - 2 * (c % 2),)

    def up(c):
        return ((c + 2) % n_ctx,)

    swapped = route(send, ["ctx"], other)
    packs = [keep, swapped]
    for _ in range(levels_back):
        packs += [route(packs[-2], ["ctx"], up), route(packs[-1], ["ctx"], up)]
    q_send = lax.dynamic_slice(queries[0], (0, (1 - side) * half_width), (rows, half_width))
    s_send = lax.dynamic_slice(stream[0], (0, (1 - side) * half_width), (rows, half_width))
    q_part = route(q_send, ["ctx"], other)
    s_part = route(s_send, ["ctx"], other)

    straight, across, own_sq, part_sq = [], [], [], []
    for stage in range(halves):
        own, part, sq_o, sq_p = pl.pallas_call(
            functools.partial(attend_kernel, stage, halves, group, levels_back),
            out_shape=[jax.ShapeDtypeStruct((rows, width), jnp.bfloat16)] * 2
            + [jax.ShapeDtypeStruct((8, HEAD), jnp.float32)] * 2,
            in_specs=[vmem] * (4 + len(packs)),
            out_specs=[vmem] * 4,
            compiler_params=params,
            name=f"attend{stage}",
        )(queries, stream, q_part, s_part, *packs)
        across.append(route(part, ["pipe", "ctx"], lambda p, c: ((p + 1) % n_pipe, *other(c))))
        straight.append(route(own, ["pipe"], lambda p: ((p + 1) % n_pipe,)))
        own_sq.append(sq_o)
        part_sq.append(sq_p)
    sq_a = route(sum(own_sq), ["pipe", "tp"], lambda p, t: ((p + 1) % n_pipe, 1 - t))
    sq_b = route(
        sum(part_sq),
        ["pipe", "ctx", "tp"],
        lambda p, c, t: ((p + 1) % n_pipe, *other(c), 1 - t),
    )
    return tuple(
        pl.pallas_call(
            functools.partial(final_kernel, halves, width),
            out_shape=[jax.ShapeDtypeStruct(stream.shape, jnp.bfloat16)] * 2,
            in_specs=[vmem] * (2 * halves + 3),
            out_specs=[vmem] * 2,
            compiler_params=params,
            name="norm",
        )(*straight, *across, sq_a, sq_b, norm_gain[None])
    )


def solution(mesh):
    spec = P("pipe", "ctx", "tp")
    return jax.shard_map(
        per_device,
        mesh=mesh,
        in_specs=(spec, spec, spec, spec, P("pipe", "ctx"), P("tp")),
        out_specs=(spec, spec),
        check_vma=False,
    )
```

time: 126 us -> 44.3 us (0.35)
  waiting for transfers between devices: 61.1 us -> 18.2 us
  blocking collectives: 22.3 us -> 0 us
  between operations: 14.1 us -> 0.7 us
  starting transfers between devices: 3.42 us -> 16.3 us
  matrix products: 9.04 us -> 0 us
  local copies, waits for them, and re-layouts: 10.3 us -> 3.59 us
  Pallas kernels: 0 us -> 5.36 us
  other arithmetic: 4.85 us -> 0.01 us
    all_gather x2 -> x0, waiting for transfers between devices: 50.4 us -> none  [the longest x1 31.8 us: per_device(): lax.all_gather(values[0], 'ctx', axis=0, tiled=True)]
    all_gather x1 -> x0, blocking collectives: 17.9 us -> none  [per_device(): lax.all_gather(segments[0], 'ctx', axis=0, tiled=True)[None, :]]
    ppermute x1 -> x13, starting transfers between devices: 3.34 us -> 16.3 us  [route(): return lax.ppermute(x, tuple(axes) if len(axes) > 1 else axes[0], pairs)]
    dot_general x2 -> x0, matrix products: 9.04 us -> none  [the longest x1 5.97 us: per_device(): jnp.einsum('hrk,khd->hrd', weights.astype(jnp.bfloat16), value_head_stack...]
    ppermute x1 -> x13, waiting for transfers between devices: 10.7 us -> 18.2 us  [route(): return lax.ppermute(x, tuple(axes) if len(axes) > 1 else axes[0], pairs)]
    pallas_call x0 -> x4, Pallas kernels: none -> 5.36 us  [the longest x2 3.97 us: per_device(): pl.pallas_call(functools.partial(attend_kernel, stage, halves, group, lev...]
    unnamed x9 -> x12, local copies, waits for them, and re-layouts: 7.33 us -> 2.52 us
    psum x1 -> x0, blocking collectives: 4.33 us -> none  [per_device(): totals = lax.psum(squares, 'tp')]
  transfers between devices with their start and end apart: 3 -> 13, of which waited for: 3 -> 7; matrix products, arithmetic and copies ran while one was open for 8% -> 2% of each run, Pallas kernels for 0% -> 4%
where the time goes in v1:
time: 44.3 us; the launch traced here: 44.1 us
  waiting for transfers between devices  18.2 us (41%)
  starting transfers between devices  16.3 us (37%)
  Pallas kernels  5.36 us (12%)
  local copies, waits for them, and re-layouts  3.59 us (8%)
  between operations  0.7 us (2%)
    ppermute x13, waiting for transfers between devices, route(): return lax.ppermute(x, tuple(axes) if len(axes) > 1 else axes[0], pairs)  18.2 us
    ppermute x13, starting transfers between devices, route(): return lax.ppermute(x, tuple(axes) if len(axes) > 1 else axes[0], pairs)  16.3 us
    pallas_call x2, Pallas kernels, per_device(): pl.pallas_call(functools.partial(attend_kernel, stage, halves, group, lev...  3.97 us
    unnamed x12, local copies, waits for them, and re-layouts  2.52 us
    pallas_call x1, Pallas kernels, per_device(): pl.pallas_call(functools.partial(final_kernel, halves, width), out_shape=...  1.34 us
    dynamic_slice x1, local copies, waits for them, and re-layouts, per_device(): lax.dynamic_slice(queries[0], (0, (1 - side) * half_width), (rows, half_w...  1.04 us
  transfers between devices with their start and end apart: 13, of which 7 were waited for; matrix products, arithmetic and copies ran while one was open for 2% of the time, Pallas kernels for 4%

profile of v1, /device:TPU:1, one launch (start us, length us, event | category | flops | bytes accessed | tf_op | source)
XLA Modules:
  0.0 44.1 jit_solution(8391699149787708870)
XLA Ops:
  0.7 1.0 %copy-done.2 = bf16[1,128,512]{2,1,0:T(8,128)(2,1)S(1)} copy-done((bf16[1,128,512]{2,1,0:T(8,128)(2,1)S(1)}, bf16[1,128,512]{2,1,0:T(8,128)(2,1)}, u32[]{:S(2)}) %copy-start.2) | copy-done | bytes 131096
  1.6 0.9 %copy-done.3 = bf16[1,128,512]{2,1,0:T(8,128)(2,1)S(1)} copy-done((bf16[1,128,512]{2,1,0:T(8,128)(2,1)S(1)}, bf16[1,128,512]{2,1,0:T(8,128)(2,1)}, u32[]{:S(2)}) %copy-start.3) | copy-done | bytes 131096
  2.5 0.7 %copy-done.4 = s32[1,128]{1,0:T(1,128)S(1)} copy-done((s32[1,128]{1,0:T(1,128)S(1)}, s32[1,128]{1,0:T(1,128)}, u32[]{:S(2)}) %copy-start.4) | copy-done | bytes 536
  3.2 0.1 pack.1
  3.2 2.1 %collective-permute-start.2 = (bf16[528,128]{1,0:T(8,128)(2,1)S(1)}, bf16[528,128]{1,0:T(8,128)(2,1)S(1)}, u32[]{:S(2)}, u32[]{:S(2)}) collective-permute-start(bf16[528,128]{1,0:T(8,128)(2,1)S(1)} %get-tuple-element.13), channel_id=1, source_target_pairs={{0,2},{2,0},{4,6},{6,4},{8,10},{10,8},{12,14},{14,12},{1,3},{3,1},... | collective-permute-start | bytes 405512 | tf_op jit(solution)/shard_map/ppermute | solution.py:31
  5.3 1.0 %dynamic-slice_bitcast_fusion.1 = bf16[128,1024]{1,0:T(8,128)(2,1)S(1)} fusion(bf16[1,128,2048]{2,1,0:T(8,128)(2,1)} %refs_0_.3, s32[]{:T(128)S(6)} %select_n.12), kind=kLoop, calls=%fused_computation.1 | loop fusion | bytes 524292 | tf_op jit(solution)/shard_map/dynamic_slice | solution.py:157
  6.4 0.1 collective-permute-start
  6.5 1.5 %collective-permute-start.3 = (bf16[528,128]{1,0:T(8,128)(2,1)S(1)}, bf16[528,128]{1,0:T(8,128)(2,1)S(1)}, u32[]{:S(2)}, u32[]{:S(2)}) collective-permute-start(bf16[528,128]{1,0:T(8,128)(2,1)S(1)} %get-tuple-element.12.refs_4_), channel_id=1, source_target_pairs={{0,4},{2,6},{4,8},{6,10},{8,12},{10,14},{12,0},{14,2},{1,5},{3,7},... | collective-permute-start | bytes 405512 | tf_op jit(solution)/shard_map/ppermute | solution.py:31
  8.0 0.6 %collective-permute-done.2.refs_5_ = bf16[528,128]{1,0:T(8,128)(2,1)S(1)} collective-permute-done((bf16[528,128]{1,0:T(8,128)(2,1)S(1)}, bf16[528,128]{1,0:T(8,128)(2,1)S(1)}, u32[]{:S(2)}, u32[]{:S(2)}) %collective-permute-start.2) | collective-permute-done | bytes 135200 | tf_op jit(solution)/shard_map/ppermute | solution.py:31
  8.6 1.2 %collective-permute-start.4 = (bf16[528,128]{1,0:T(8,128)(2,1)S(1)}, bf16[528,128]{1,0:T(8,128)(2,1)S(1)}, u32[]{:S(2)}, u32[]{:S(2)}) collective-permute-start(bf16[528,128]{1,0:T(8,128)(2,1)S(1)} %collective-permute-done.2.refs_5_), channel_id=1, source_target_pairs={{0,4},{2,6},{4,8},{6,10},{8,12},{10,14},{12,0},{14,2},{1,5},{3,7},... | collective-permute-start | bytes 405512 | tf_op jit(solution)/shard_map/ppermute | solution.py:31
  9.9 1.3 %collective-permute-start.1 = (bf16[128,1024]{1,0:T(8,128)(2,1)S(1)}, bf16[128,1024]{1,0:T(8,128)(2,1)S(1)}, u32[]{:S(2)}, u32[]{:S(2)}) collective-permute-start(bf16[128,1024]{1,0:T(8,128)(2,1)S(1)} %dynamic-slice_bitcast_fusion), channel_id=1, source_target_pairs={{0,2},{2,0},{4,6},{6,4},{8,10},{10,8},{12,14},{14,12},{1,3},{3,1},... | collective-permute-start | bytes 786440 | tf_op jit(solution)/shard_map/ppermute | solution.py:31
  11.2 1.2 %collective-permute-done.3.refs_6_ = bf16[528,128]{1,0:T(8,128)(2,1)S(1)} collective-permute-done((bf16[528,128]{1,0:T(8,128)(2,1)S(1)}, bf16[528,128]{1,0:T(8,128)(2,1)S(1)}, u32[]{:S(2)}, u32[]{:S(2)}) %collective-permute-start.3) | collective-permute-done | bytes 135200 | tf_op jit(solution)/shard_map/ppermute | solution.py:31
  12.4 0.1 collective-permute-start.5
  12.5 3.3 %collective-permute-done.4.refs_7_ = bf16[528,128]{1,0:T(8,128)(2,1)S(1)} collective-permute-done((bf16[528,128]{1,0:T(8,128)(2,1)S(1)}, bf16[528,128]{1,0:T(8,128)(2,1)S(1)}, u32[]{:S(2)}, u32[]{:S(2)}) %collective-permute-start.4) | collective-permute-done | bytes 135200 | tf_op jit(solution)/shard_map/ppermute | solution.py:31
  15.7 0.0 collective-permute-start.6
  15.7 0.0 collective-permute-done.refs_2_
  15.7 3.8 %collective-permute-done.1.refs_3_ = bf16[128,1024]{1,0:T(8,128)(2,1)S(1)} collective-permute-done((bf16[128,1024]{1,0:T(8,128)(2,1)S(1)}, bf16[128,1024]{1,0:T(8,128)(2,1)S(1)}, u32[]{:S(2)}, u32[]{:S(2)}) %collective-permute-start.1) | collective-permute-done | bytes 262176 | tf_op jit(solution)/shard_map/ppermute | solution.py:31
  19.6 0.0 collective-permute-done.5.refs_8_
  19.6 3.3 %collective-permute-done.6.refs_9_ = bf16[528,128]{1,0:T(8,128)(2,1)S(1)} collective-permute-done((bf16[528,128]{1,0:T(8,128)(2,1)S(1)}, bf16[528,128]{1,0:T(8,128)(2,1)S(1)}, u32[]{:S(2)}, u32[]{:S(2)}) %collective-permute-start.6) | collective-permute-done | bytes 135200 | tf_op jit(solution)/shard_map/ppermute | solution.py:31
  22.8 2.0 %attend1.1 = (bf16[128,512]{1,0:T(8,128)(2,1)S(1)}, bf16[128,512]{1,0:T(8,128)(2,1)S(1)}, f32[8,128]{1,0:T(8,128)S(1)}, f32[8,128]{1,0:T(8,128)S(1)}) custom-call(bf16[1,128,2048]{2,1,0:T(8,128)(2,1)S(1)} %copy-done, bf16[1,128,2048]{2,1,0:T(8,128)(2,1)S(1)} %copy-done.1, bf16[128,1024]{1,0:T(8,128)(2,1)S(1)} %collective-permute-done.refs_2_, ...), custom_call_target="tpu_custom_call" | custom-call | tf_op jit(solution)/shard_map/attend1/pallas_call | solution.py:164
  24.8 1.5 %collective-permute-start.10 = (bf16[128,512]{1,0:T(8,128)(2,1)S(1)}, bf16[128,512]{1,0:T(8,128)(2,1)S(1)}, u32[]{:S(2)}, u32[]{:S(2)}) collective-permute-start(bf16[128,512]{1,0:T(8,128)(2,1)S(1)} %get-tuple-element.17), channel_id=1, source_target_pairs={{0,18},{2,16},{4,22},{6,20},{8,26},{10,24},{12,30},{14,28},{16,2},... | collective-permute-start | bytes 393224 | tf_op jit(solution)/shard_map/ppermute | solution.py:31
  26.3 0.2 collective-permute-start.8
  26.6 2.0 %attend0.1 = (bf16[128,512]{1,0:T(8,128)(2,1)S(1)}, bf16[128,512]{1,0:T(8,128)(2,1)S(1)}, f32[8,128]{1,0:T(8,128)S(1)}, f32[8,128]{1,0:T(8,128)S(1)}) custom-call(bf16[1,128,2048]{2,1,0:T(8,128)(2,1)S(1)} %copy-done, bf16[1,128,2048]{2,1,0:T(8,128)(2,1)S(1)} %copy-done.1, bf16[128,1024]{1,0:T(8,128)(2,1)S(1)} %collective-permute-done.refs_2_, ...), custom_call_target="tpu_custom_call" | custom-call | tf_op jit(solution)/shard_map/attend0/pallas_call | solution.py:164
  28.5 1.3 %collective-permute-start.7 = (bf16[128,512]{1,0:T(8,128)(2,1)S(1)}, bf16[128,512]{1,0:T(8,128)(2,1)S(1)}, u32[]{:S(2)}, u32[]{:S(2)}) collective-permute-start(bf16[128,512]{1,0:T(8,128)(2,1)S(1)} %get-tuple-element.14), channel_id=1, source_target_pairs={{0,16},{16,0},{1,17},{17,1},{2,18},{18,2},{3,19},{19,3},{4,20},{20... | collective-permute-start | bytes 393224 | tf_op jit(solution)/shard_map/ppermute | solution.py:31
  29.8 0.9 %collective-permute-start.9 = (bf16[128,512]{1,0:T(8,128)(2,1)S(1)}, bf16[128,512]{1,0:T(8,128)(2,1)S(1)}, u32[]{:S(2)}, u32[]{:S(2)}) collective-permute-start(bf16[128,512]{1,0:T(8,128)(2,1)S(1)} %get-tuple-element.16), channel_id=1, source_target_pairs={{0,18},{2,16},{4,22},{6,20},{8,26},{10,24},{12,30},{14,28},{16,2},... | collective-permute-start | bytes 393224 | tf_op jit(solution)/shard_map/ppermute | solution.py:31
  30.8 6.0 %collective-permute-start.12 = (f32[8,128]{1,0:T(8,128)S(1)}, f32[8,128]{1,0:T(8,128)S(1)}, u32[]{:S(2)}, u32[]{:S(2)}) collective-permute-start(f32[8,128]{1,0:T(8,128)S(1)} %add.17), channel_id=1, source_target_pairs={{0,19},{1,18},{2,17},{3,16},{4,23},{5,22},{6,21},{7,20},{8,27},{9,... | collective-permute-start | bytes 12296 | tf_op jit(solution)/shard_map/ppermute | solution.py:31
  36.8 2.9 %collective-permute-done.12.refs_5_ = f32[8,128]{1,0:T(8,128)S(1)} collective-permute-done((f32[8,128]{1,0:T(8,128)S(1)}, f32[8,128]{1,0:T(8,128)S(1)}, u32[]{:S(2)}, u32[]{:S(2)}) %collective-permute-start.12) | collective-permute-done | bytes 4128 | tf_op jit(solution)/shard_map/ppermute | solution.py:31
  39.7 3.0 %collective-permute-done.11.refs_4_ = f32[8,128]{1,0:T(8,128)S(1)} collective-permute-done((f32[8,128]{1,0:T(8,128)S(1)}, f32[8,128]{1,0:T(8,128)S(1)}, u32[]{:S(2)}, u32[]{:S(2)}) %collective-permute-start.11) | collective-permute-done | bytes 4128 | tf_op jit(solution)/shard_map/ppermute | solution.py:31
  42.8 0.0 collective-permute-done.10.refs_3_
  42.8 0.0 collective-permute-done.8.refs_1_
  42.8 0.0 collective-permute-done.7.refs_0_
  42.8 1.3 %norm.1 = (bf16[1,128,2048]{2,1,0:T(8,128)(2,1)}, bf16[1,128,2048]{2,1,0:T(8,128)(2,1)}) custom-call(bf16[128,512]{1,0:T(8,128)(2,1)S(1)} %collective-permute-done.7.refs_0_, bf16[128,512]{1,0:T(8,128)(2,1)S(1)} %collective-permute-done.8.refs_1_, bf16[128,512]{1,0:T(8,128)(2,1)S(1)} %collective-permute-done.9.refs_2_, ...), custom_call_target="tpu_custom_call" | custom-call | tf_op jit(solution)/shard_map/norm/pallas_call | solution.py:184
  (15 shorter events, 0.1 us)
Async XLA Ops:
  0.6 9.2 %copy-start.1 = (bf16[1,128,2048]{2,1,0:T(8,128)(2,1)S(1)}, bf16[1,128,2048]{2,1,0:T(8,128)(2,1)}, u32[]{:S(2)}) copy-start(bf16[1,128,2048]{2,1,0:T(8,128)(2,1)} %refs_1_.3) | copy-start | bytes 1572868
  0.6 1.0 %copy-start.2 = (bf16[1,128,512]{2,1,0:T(8,128)(2,1)S(1)}, bf16[1,128,512]{2,1,0:T(8,128)(2,1)}, u32[]{:S(2)}) copy-start(bf16[1,128,512]{2,1,0:T(8,128)(2,1)} %k_ref.1) | copy-start | bytes 393220
  1.6 0.9 %copy-start.3 = (bf16[1,128,512]{2,1,0:T(8,128)(2,1)S(1)}, bf16[1,128,512]{2,1,0:T(8,128)(2,1)}, u32[]{:S(2)}) copy-start(bf16[1,128,512]{2,1,0:T(8,128)(2,1)} %v_ref.1) | copy-start | bytes 393220
  2.5 0.7 %copy-start.4 = (s32[1,128]{1,0:T(1,128)S(1)}, s32[1,128]{1,0:T(1,128)}, u32[]{:S(2)}) copy-start(s32[1,128]{1,0:T(1,128)} %seg_ref.1) | copy-start | bytes 1540
  3.2 5.4 %collective-permute-start.2 = (bf16[528,128]{1,0:T(8,128)(2,1)S(1)}, bf16[528,128]{1,0:T(8,128)(2,1)S(1)}, u32[]{:S(2)}, u32[]{:S(2)}) collective-permute-start(bf16[528,128]{1,0:T(8,128)(2,1)S(1)} %get-tuple-element.13), channel_id=1, source_target_pairs={{0,2},{2,0},{4,6},{6,4},{8,10},{10,8},{12,14},{14,12},{1,3},{3,1},... | collective-permute-start | bytes 405512 | tf_op jit(solution)/shard_map/ppermute | solution.py:31
  5.3 17.5 %copy-start = (bf16[1,128,2048]{2,1,0:T(8,128)(2,1)S(1)}, bf16[1,128,2048]{2,1,0:T(8,128)(2,1)}, u32[]{:S(2)}) copy-start(bf16[1,128,2048]{2,1,0:T(8,128)(2,1)} %refs_0_.3) | copy-start | bytes 1572868
  6.4 9.4 %collective-permute-start = (bf16[128,1024]{1,0:T(8,128)(2,1)S(1)}, bf16[128,1024]{1,0:T(8,128)(2,1)S(1)}, u32[]{:S(2)}, u32[]{:S(2)}) collective-permute-start(bf16[128,1024]{1,0:T(8,128)(2,1)S(1)} %dynamic-slice_bitcast_fusion.1), channel_id=1, source_target_pairs={{0,2},{2,0},{4,6},{6,4},{8,10},{10,8},{12,14},{14,12},{1,3},{3,1},... | collective-permute-start | bytes 786440 | tf_op jit(solution)/shard_map/ppermute | solution.py:31
  6.5 5.9 %collective-permute-start.3 = (bf16[528,128]{1,0:T(8,128)(2,1)S(1)}, bf16[528,128]{1,0:T(8,128)(2,1)S(1)}, u32[]{:S(2)}, u32[]{:S(2)}) collective-permute-start(bf16[528,128]{1,0:T(8,128)(2,1)S(1)} %get-tuple-element.12.refs_4_), channel_id=1, source_target_pairs={{0,4},{2,6},{4,8},{6,10},{8,12},{10,14},{12,0},{14,2},{1,5},{3,7},... | collective-permute-start | bytes 405512 | tf_op jit(solution)/shard_map/ppermute | solution.py:31
  8.6 7.1 %collective-permute-start.4 = (bf16[528,128]{1,0:T(8,128)(2,1)S(1)}, bf16[528,128]{1,0:T(8,128)(2,1)S(1)}, u32[]{:S(2)}, u32[]{:S(2)}) collective-permute-start(bf16[528,128]{1,0:T(8,128)(2,1)S(1)} %collective-permute-done.2.refs_5_), channel_id=1, source_target_pairs={{0,4},{2,6},{4,8},{6,10},{8,12},{10,14},{12,0},{14,2},{1,5},{3,7},... | collective-permute-start | bytes 405512 | tf_op jit(solution)/shard_map/ppermute | solution.py:31
  9.9 9.7 %collective-permute-start.1 = (bf16[128,1024]{1,0:T(8,128)(2,1)S(1)}, bf16[128,1024]{1,0:T(8,128)(2,1)S(1)}, u32[]{:S(2)}, u32[]{:S(2)}) collective-permute-start(bf16[128,1024]{1,0:T(8,128)(2,1)S(1)} %dynamic-slice_bitcast_fusion), channel_id=1, source_target_pairs={{0,2},{2,0},{4,6},{6,4},{8,10},{10,8},{12,14},{14,12},{1,3},{3,1},... | collective-permute-start | bytes 786440 | tf_op jit(solution)/shard_map/ppermute | solution.py:31
  12.4 7.2 %collective-permute-start.5 = (bf16[528,128]{1,0:T(8,128)(2,1)S(1)}, bf16[528,128]{1,0:T(8,128)(2,1)S(1)}, u32[]{:S(2)}, u32[]{:S(2)}) collective-permute-start(bf16[528,128]{1,0:T(8,128)(2,1)S(1)} %collective-permute-done.3.refs_6_), channel_id=1, source_target_pairs={{0,4},{2,6},{4,8},{6,10},{8,12},{10,14},{12,0},{14,2},{1,5},{3,7},... | collective-permute-start | bytes 405512 | tf_op jit(solution)/shard_map/ppermute | solution.py:31
  15.7 7.1 %collective-permute-start.6 = (bf16[528,128]{1,0:T(8,128)(2,1)S(1)}, bf16[528,128]{1,0:T(8,128)(2,1)S(1)}, u32[]{:S(2)}, u32[]{:S(2)}) collective-permute-start(bf16[528,128]{1,0:T(8,128)(2,1)S(1)} %collective-permute-done.4.refs_7_), channel_id=1, source_target_pairs={{0,4},{2,6},{4,8},{6,10},{8,12},{10,14},{12,0},{14,2},{1,5},{3,7},... | collective-permute-start | bytes 405512 | tf_op jit(solution)/shard_map/ppermute | solution.py:31
  24.8 17.9 %collective-permute-start.10 = (bf16[128,512]{1,0:T(8,128)(2,1)S(1)}, bf16[128,512]{1,0:T(8,128)(2,1)S(1)}, u32[]{:S(2)}, u32[]{:S(2)}) collective-permute-start(bf16[128,512]{1,0:T(8,128)(2,1)S(1)} %get-tuple-element.17), channel_id=1, source_target_pairs={{0,18},{2,16},{4,22},{6,20},{8,26},{10,24},{12,30},{14,28},{16,2},... | collective-permute-start | bytes 393224 | tf_op jit(solution)/shard_map/ppermute | solution.py:31
  26.3 16.4 %collective-permute-start.8 = (bf16[128,512]{1,0:T(8,128)(2,1)S(1)}, bf16[128,512]{1,0:T(8,128)(2,1)S(1)}, u32[]{:S(2)}, u32[]{:S(2)}) collective-permute-start(bf16[128,512]{1,0:T(8,128)(2,1)S(1)} %get-tuple-element.15), channel_id=1, source_target_pairs={{0,16},{16,0},{1,17},{17,1},{2,18},{18,2},{3,19},{19,3},{4,20},{20... | collective-permute-start | bytes 393224 | tf_op jit(solution)/shard_map/ppermute | solution.py:31
  28.5 14.2 %collective-permute-start.7 = (bf16[128,512]{1,0:T(8,128)(2,1)S(1)}, bf16[128,512]{1,0:T(8,128)(2,1)S(1)}, u32[]{:S(2)}, u32[]{:S(2)}) collective-permute-start(bf16[128,512]{1,0:T(8,128)(2,1)S(1)} %get-tuple-element.14), channel_id=1, source_target_pairs={{0,16},{16,0},{1,17},{17,1},{2,18},{18,2},{3,19},{19,3},{4,20},{20... | collective-permute-start | bytes 393224 | tf_op jit(solution)/shard_map/ppermute | solution.py:31
  29.8 12.9 %collective-permute-start.9 = (bf16[128,512]{1,0:T(8,128)(2,1)S(1)}, bf16[128,512]{1,0:T(8,128)(2,1)S(1)}, u32[]{:S(2)}, u32[]{:S(2)}) collective-permute-start(bf16[128,512]{1,0:T(8,128)(2,1)S(1)} %get-tuple-element.16), channel_id=1, source_target_pairs={{0,18},{2,16},{4,22},{6,20},{8,26},{10,24},{12,30},{14,28},{16,2},... | collective-permute-start | bytes 393224 | tf_op jit(solution)/shard_map/ppermute | solution.py:31
  30.8 8.9 %collective-permute-start.12 = (f32[8,128]{1,0:T(8,128)S(1)}, f32[8,128]{1,0:T(8,128)S(1)}, u32[]{:S(2)}, u32[]{:S(2)}) collective-permute-start(f32[8,128]{1,0:T(8,128)S(1)} %add.17), channel_id=1, source_target_pairs={{0,19},{1,18},{2,17},{3,16},{4,23},{5,22},{6,21},{7,20},{8,27},{9,... | collective-permute-start | bytes 12296 | tf_op jit(solution)/shard_map/ppermute | solution.py:31
  36.8 2.9 %copy-start.5 = (bf16[2048]{0:T(1024)(128)(2,1)S(1)}, bf16[2048]{0:T(1024)(128)(2,1)}, u32[]{:S(2)}) copy-start(bf16[2048]{0:T(1024)(128)(2,1)} %param.11) | copy-start | bytes 12292
  39.7 3.0 %collective-permute-start.11 = (f32[8,128]{1,0:T(8,128)S(1)}, f32[8,128]{1,0:T(8,128)S(1)}, u32[]{:S(2)}, u32[]{:S(2)}) collective-permute-start(f32[8,128]{1,0:T(8,128)S(1)} %add.16), channel_id=1, source_target_pairs={{0,17},{1,16},{16,1},{17,0},{2,19},{3,18},{18,3},{19,2},{4,21},{5,... | collective-permute-start | bytes 12296 | tf_op jit(solution)/shard_map/ppermute | solution.py:31

commit v2 on v1

v2 whole, which is shorter than its diff:
```python
import functools
import math

import jax
import jax.numpy as jnp
from jax import lax
from jax.experimental import pallas as pl
from jax.experimental.pallas import tpu as pltpu
from jax.sharding import PartitionSpec as P

HEAD = 128
FEATURES = 4096
EPS = 1e-05
SEG_ROWS = 16
NEG = -1e30
VMEM_LIMIT = 40 * 1024 * 1024


def route(x, axes, move):
    sizes = [lax.axis_size(a) for a in axes]
    pairs = []
    for src in range(math.prod(sizes)):
        at, rest = [], src
        for s in reversed(sizes):
            at.insert(0, rest % s)
            rest //= s
        target = move(*at)
        if target is not None:
            to = 0
            for s, v in zip(sizes, target):
                to = to * s + v
            pairs.append((src, to))
    return lax.ppermute(x, tuple(axes) if len(axes) > 1 else axes[0], pairs)


def gate(x, *earlier):
    return pl.pallas_call(
        lambda *refs: None,
        out_shape=jax.ShapeDtypeStruct(x.shape, x.dtype),
        in_specs=[pl.BlockSpec(memory_space=pl.ANY)] * (1 + len(earlier)),
        out_specs=pl.BlockSpec(memory_space=pl.ANY),
        input_output_aliases={0: 0},
        compiler_params=pltpu.CompilerParams(vmem_limit_bytes=VMEM_LIMIT),
        name="gate",
    )(x, *earlier)


def turned(row):
    return jnp.transpose(jnp.broadcast_to(row, (HEAD, HEAD)))


class Fetches:
    def __init__(self, sems):
        self.sems, self.copies = sems, []

    def start(self, src, dst):
        self.copies.append(pltpu.make_async_copy(src, dst, self.sems.at[len(self.copies)]))
        self.copies[-1].start()

    def wait(self):
        for c in self.copies:
            c.wait()


def lanes(start, size):
    return pl.ds(pl.multiple_of(start * HEAD, HEAD), size * HEAD)


def pack_kernel(halves, tiles, k_ref, v_ref, seg_ref, q_ref, s_ref, keep, send, far, seg_buf, sems):
    side = lax.axis_index("ctx") % 2
    fetches = Fetches(sems)
    fetches.start(seg_ref, seg_buf)
    for out, half in ((keep, side), (send, 1 - side)):
        for h in range(halves):
            for n, ref in enumerate((k_ref, v_ref)):
                rows = pl.ds((2 * h + n) * HEAD, HEAD)
                fetches.start(ref.at[0, :, lanes(half * halves + h, 1)], out.at[rows])
    for n, ref in enumerate((q_ref, s_ref)):
        fetches.start(ref.at[0, :, lanes((1 - side) * tiles, tiles)], far.at[n])
    fetches.wait()
    seg = jnp.broadcast_to(seg_buf[...], (SEG_ROWS, HEAD)).astype(jnp.float32).astype(jnp.bfloat16)
    for out in (keep, send):
        out[2 * halves * HEAD :, :] = seg


def attend_kernel(own, halves, group, q_ref, s_ref, *refs):
    *packs, out, out_sq = refs
    rows = HEAD
    ctx = lax.axis_index("ctx")
    side = ctx % 2
    own_pos, part_pos = ctx * rows, (ctx + 1 - 2 * side) * rows
    seg_at = 2 * halves * HEAD

    def seg_of(pack):
        return pack[seg_at : seg_at + SEG_ROWS, :].astype(jnp.float32)[:1]

    lane = lax.broadcasted_iota(jnp.int32, (rows, rows), 1)
    line = lax.broadcasted_iota(jnp.int32, (rows, rows), 0)
    q_start, q_seg = (own_pos, packs[0]) if own else (part_pos, packs[1])
    q_seg = turned(seg_of(q_seg))
    tiles = []
    for n, pack in enumerate(packs):
        k_start = (own_pos, part_pos)[n % 2] - (n // 2) * 2 * rows
        ok = (lane + k_start <= line + q_start) & (lane + k_start >= 0)
        ok &= q_seg == jnp.broadcast_to(seg_of(pack), (rows, rows))
        tiles.append(jnp.where(ok, 0.0, NEG))
    bias = jnp.concatenate(tiles, axis=1)
    scale = HEAD ** (-0.5) * math.log2(math.e)
    sq = jnp.zeros((rows, HEAD), jnp.float32)
    for h in range(halves):
        at = 2 * h * HEAD
        keys = jnp.concatenate([p[at : at + HEAD, :] for p in packs], axis=0)
        vals = jnp.concatenate([p[at + HEAD : at + 2 * HEAD, :] for p in packs], axis=0)
        here = [h * group + g for g in range(group)]
        if own:
            q = [q_ref[0, :, lanes(side * halves * group + n, 1)] for n in here]
        else:
            q = [q_ref[0, :, n * HEAD : (n + 1) * HEAD] for n in here]
        s = lax.dot_general(
            jnp.concatenate(q, axis=0),
            keys,
            (((1,), (1,)), ((), ())),
            preferred_element_type=jnp.float32,
        )
        s = s.reshape(group, rows, -1) * scale + bias[None]
        w = jnp.exp2(s - jnp.max(s, axis=2, keepdims=True))
        total = jnp.sum(w, axis=2, keepdims=True)
        w = w.astype(jnp.bfloat16).reshape(group * rows, -1)
        att = jnp.dot(w, vals, preferred_element_type=jnp.float32).reshape(group, rows, HEAD) / total
        att = att.astype(jnp.bfloat16).astype(jnp.float32)
        for g, n in enumerate(here):
            if own:
                stream = s_ref[0, :, lanes(side * halves * group + n, 1)]
            else:
                stream = s_ref[1, :, n * HEAD : (n + 1) * HEAD]
            adv = (stream.astype(jnp.float32) + att[g]).astype(jnp.bfloat16)
            out[:, n * HEAD : (n + 1) * HEAD] = adv
            sq += adv.astype(jnp.float32) ** 2
    out_sq[...] = row_sums(sq)


def row_sums(sq):
    return jnp.broadcast_to(jnp.sum(jnp.transpose(sq), axis=0, keepdims=True), (8, HEAD))


def final_kernel(tiles, own, part, sq_a, sq_b, gain_ref, arrived_ref, normed_ref):
    side = lax.axis_index("ctx") % 2
    sq = jnp.zeros((HEAD, HEAD), jnp.float32)
    for p in (own, part):
        for n in range(tiles):
            sq += p[:, n * HEAD : (n + 1) * HEAD].astype(jnp.float32) ** 2
    total = (row_sums(sq) + sq_a[...] + sq_b[...])[:1]
    inv = turned(lax.rsqrt(total / FEATURES + EPS))
    for half, p in ((side, own), (1 - side, part)):
        for n in range(tiles):
            a = p[:, n * HEAD : (n + 1) * HEAD]
            at = lanes(half * tiles + n, 1)
            arrived_ref[0, :, at] = a
            gain = gain_ref[:, at].astype(jnp.float32)
            normed_ref[0, :, at] = (a.astype(jnp.float32) * inv * gain).astype(jnp.bfloat16)


def per_device(stream, queries, keys, values, segments, norm_gain):
    rows = stream.shape[1]
    halves = keys.shape[2] // HEAD // 2
    group = queries.shape[2] // keys.shape[2]
    tiles = halves * group
    n_ctx = lax.axis_size("ctx")
    n_pipe = lax.axis_size("pipe")
    level = 2 * rows
    levels_back = (n_ctx * rows // 2 - 1 + level - 1) // level
    vmem = pl.BlockSpec(memory_space=pltpu.VMEM)
    anywhere = pl.BlockSpec(memory_space=pl.ANY)
    params = pltpu.CompilerParams(vmem_limit_bytes=VMEM_LIMIT)
    sums = jax.ShapeDtypeStruct((8, HEAD), jnp.float32)

    def other(c):
        return c + 1 - 2 * (c % 2)

    def up(c):
        return (c + 2) % n_ctx

    def after(p):
        return (p + 1) % n_pipe

    def hop(p, c, distance):
        z, x = c // 2, c % 2
        if z < distance:
            return after(p), c
        return p, 2 * (z + 1 if 2 * z + 2 < n_ctx else distance) + x

    def buffer(*shape):
        return jax.ShapeDtypeStruct(shape, jnp.bfloat16)

    def held(x):
        return pltpu.with_memory_space_constraint(x, pltpu.HBM)

    keep, send, far = pl.pallas_call(
        functools.partial(pack_kernel, halves, tiles),
        out_shape=[buffer(2 * halves * HEAD + SEG_ROWS, HEAD)] * 2 + [buffer(2, rows, tiles * HEAD)],
        in_specs=[anywhere] * 5,
        out_specs=[vmem] * 3,
        scratch_shapes=[pltpu.VMEM((1, rows), jnp.int32), pltpu.SemaphoreType.DMA((3 + 4 * halves,))],
        compiler_params=params,
        name="pack",
    )(*(held(x) for x in (keys, values, segments, queries, stream)))
    packs = [
        keep,
        route(send, ["ctx"], lambda c: (other(c),)),
        route(keep, ["ctx"], lambda c: (up(c),)),
        route(send, ["ctx"], lambda c: (up(other(c)),)),
    ]
    far = route(gate(far, packs[1]), ["ctx"], lambda c: (other(c),))
    for n in range(1, levels_back):
        packs += [route(b, ["pipe", "ctx"], lambda p, c: hop(p, c, n)) for b in packs[-2:]]
    def attend(own, q, s):
        return pl.pallas_call(
            functools.partial(attend_kernel, own, halves, group),
            out_shape=[buffer(rows, tiles * HEAD), sums],
            in_specs=[vmem] * (2 + len(packs)),
            out_specs=[vmem] * 2,
            compiler_params=params,
            cost_estimate=pl.CostEstimate(flops=3000000000 if own else 1000000000, bytes_accessed=0, transcendentals=0),
            name="attend_own" if own else "attend_part",
        )(q, s, *packs)

    own, own_sq = attend(True, queries, stream)
    straight = route(own, ["pipe"], lambda p: (after(p),))
    sq_a = route(own_sq, ["pipe", "tp"], lambda p, t: (after(p), 1 - t))
    far = gate(far, own)
    part, part_sq = attend(False, far, far)
    across = route(part, ["pipe", "ctx"], lambda p, c: (after(p), other(c)))
    sq_b = route(part_sq, ["pipe", "ctx", "tp"], lambda p, c, t: (after(p), other(c), 1 - t))
    return tuple(
        pl.pallas_call(
            functools.partial(final_kernel, tiles),
            out_shape=[buffer(*stream.shape)] * 2,
            in_specs=[vmem] * 5,
            out_specs=[vmem] * 2,
            compiler_params=params,
            name="norm",
        )(straight, across, sq_a, sq_b, norm_gain[None])
    )


def solution(mesh):
    spec = P("pipe", "ctx", "tp")
    return jax.shard_map(
        per_device,
        mesh=mesh,
        in_specs=(spec, spec, spec, spec, P("pipe", "ctx"), P("tp")),
        out_specs=(spec, spec),
        check_vma=False,
    )
```

time: 44.3 us -> 36.4 us (0.82)
  local copies, waits for them, and re-layouts: 3.59 us -> 0.02 us
  waiting for transfers between devices: 18.2 us -> 15.2 us
  starting transfers between devices: 16.3 us -> 13.8 us
  Pallas kernels: 5.36 us -> 6.18 us
    ppermute x13 -> x10, waiting for transfers between devices: 18.2 us -> 15.2 us  [route(): return lax.ppermute(x, tuple(axes) if len(axes) > 1 else axes[0], pairs)]
    unnamed x12 -> x6, local copies, waits for them, and re-layouts: 2.52 us -> 0.01 us
    ppermute x13 -> x10, starting transfers between devices: 16.3 us -> 13.8 us  [route(): return lax.ppermute(x, tuple(axes) if len(axes) > 1 else axes[0], pairs)]
    dynamic_slice x2 -> x0, local copies, waits for them, and re-layouts: 1.06 us -> none  [the longest x1 1.04 us: per_device(): lax.dynamic_slice(queries[0], (0, (1 - side) * half_width), (rows, half_w...]
    pallas_call x4 -> x6, Pallas kernels: 5.36 us -> 6.18 us  [the longest x2 3.53 us: attend(): pl.pallas_call(functools.partial(attend_kernel, own, halves, group), out_...]
  transfers between devices with their start and end apart: 13 -> 10, of which waited for: 7 -> 6; matrix products, arithmetic and copies ran while one was open for 2% -> 0% of each run, Pallas kernels for 4% -> 10%
where the time goes in v2:
time: 36.4 us; the launch traced here: 35.9 us
  waiting for transfers between devices  15.2 us (42%)
  starting transfers between devices  13.8 us (38%)
  Pallas kernels  6.18 us (17%)
  between operations  0.67 us (2%)
    ppermute x10, waiting for transfers between devices, route(): return lax.ppermute(x, tuple(axes) if len(axes) > 1 else axes[0], pairs)  15.2 us
    ppermute x10, starting transfers between devices, route(): return lax.ppermute(x, tuple(axes) if len(axes) > 1 else axes[0], pairs)  13.8 us
    pallas_call x2, Pallas kernels, attend(): pl.pallas_call(functools.partial(attend_kernel, own, halves, group), out_...  3.53 us
    pallas_call x1, Pallas kernels, per_device(): pl.pallas_call(functools.partial(final_kernel, tiles), out_shape=[buffer(...  1.34 us
    pallas_call x1, Pallas kernels, per_device(): pl.pallas_call(functools.partial(pack_kernel, halves, tiles), out_shape=[...  1.31 us
  transfers between devices with their start and end apart: 10, of which 6 were waited for; matrix products, arithmetic and copies ran while one was open for 0% of the time, Pallas kernels for 10%

profile of v2, /device:TPU:1, one launch (start us, length us, event | category | flops | bytes accessed | tf_op | source)
XLA Modules:
  0.0 35.9 jit_solution(8836640968146302787)
XLA Ops:
  0.6 1.3 %pack.1 = (bf16[528,128]{1,0:T(8,128)(2,1)S(1)}, bf16[528,128]{1,0:T(8,128)(2,1)S(1)}, bf16[2,128,1024]{2,1,0:T(8,128)(2,1)S(1)}) custom-call(bf16[1,128,512]{2,1,0:T(8,128)(2,1)} %k_ref.1, bf16[1,128,512]{2,1,0:T(8,128)(2,1)} %v_ref.1, s32[1,128]{1,0:T(1,128)} %seg_ref.1, bf16[1,128,2048]{2,1,0:T(8,128)(2,1)} %q_ref.3, bf16[1,128,2048]{2,1,0:T(8,128)(2,1)} %s_ref.3), custom_call_target="tpu_custom_call" | custom-call | tf_op jit(solution)/shard_map/pack/pallas_call | solution.py:198
  1.9 2.1 %collective-permute-start = (bf16[528,128]{1,0:T(8,128)(2,1)S(1)}, bf16[528,128]{1,0:T(8,128)(2,1)S(1)}, u32[]{:S(2)}, u32[]{:S(2)}) collective-permute-start(bf16[528,128]{1,0:T(8,128)(2,1)S(1)} %get-tuple-element.10), channel_id=1, source_target_pairs={{0,2},{2,0},{4,6},{6,4},{8,10},{10,8},{12,14},{14,12},{1,3},{3,1},... | collective-permute-start | bytes 405512 | tf_op jit(solution)/shard_map/ppermute | solution.py:33
  4.1 1.3 %collective-permute-start.1 = (bf16[528,128]{1,0:T(8,128)(2,1)S(1)}, bf16[528,128]{1,0:T(8,128)(2,1)S(1)}, u32[]{:S(2)}, u32[]{:S(2)}) collective-permute-start(bf16[528,128]{1,0:T(8,128)(2,1)S(1)} %get-tuple-element.9.refs_0_), channel_id=1, source_target_pairs={{0,4},{2,6},{4,8},{6,10},{8,12},{10,14},{12,0},{14,2},{1,5},{3,7},... | collective-permute-start | bytes 405512 | tf_op jit(solution)/shard_map/ppermute | solution.py:33
  5.4 1.3 %collective-permute-start.2 = (bf16[528,128]{1,0:T(8,128)(2,1)S(1)}, bf16[528,128]{1,0:T(8,128)(2,1)S(1)}, u32[]{:S(2)}, u32[]{:S(2)}) collective-permute-start(bf16[528,128]{1,0:T(8,128)(2,1)S(1)} %get-tuple-element.10), channel_id=1, source_target_pairs={{0,6},{2,4},{4,10},{6,8},{8,14},{10,12},{12,2},{14,0},{1,7},{3,5},... | collective-permute-start | bytes 405512 | tf_op jit(solution)/shard_map/ppermute | solution.py:33
  6.6 0.7 %collective-permute-done.refs_1_ = bf16[528,128]{1,0:T(8,128)(2,1)S(1)} collective-permute-done((bf16[528,128]{1,0:T(8,128)(2,1)S(1)}, bf16[528,128]{1,0:T(8,128)(2,1)S(1)}, u32[]{:S(2)}, u32[]{:S(2)}) %collective-permute-start) | collective-permute-done | bytes 135200 | tf_op jit(solution)/shard_map/ppermute | solution.py:33
  7.4 0.0 copy-start
  7.4 0.0 copy-start.1
  7.4 1.1 %collective-permute-start.6 = (bf16[2,128,1024]{2,1,0:T(8,128)(2,1)S(1)}, bf16[2,128,1024]{2,1,0:T(8,128)(2,1)S(1)}, u32[]{:S(2)}, u32[]{:S(2)}) collective-permute-start(bf16[2,128,1024]{2,1,0:T(8,128)(2,1)S(1)} %gate.2), channel_id=1, source_target_pairs={{0,2},{2,0},{4,6},{6,4},{8,10},{10,8},{12,14},{14,12},{1,3},{3,1},... | collective-permute-start | bytes 1572872 | tf_op jit(solution)/shard_map/ppermute | solution.py:33
  8.5 1.6 %collective-permute-done.1.refs_2_ = bf16[528,128]{1,0:T(8,128)(2,1)S(1)} collective-permute-done((bf16[528,128]{1,0:T(8,128)(2,1)S(1)}, bf16[528,128]{1,0:T(8,128)(2,1)S(1)}, u32[]{:S(2)}, u32[]{:S(2)}) %collective-permute-start.1) | collective-permute-done | bytes 135200 | tf_op jit(solution)/shard_map/ppermute | solution.py:33
  10.1 1.2 %collective-permute-start.3 = (bf16[528,128]{1,0:T(8,128)(2,1)S(1)}, bf16[528,128]{1,0:T(8,128)(2,1)S(1)}, u32[]{:S(2)}, u32[]{:S(2)}) collective-permute-start(bf16[528,128]{1,0:T(8,128)(2,1)S(1)} %collective-permute-done.1.refs_2_), channel_id=1, source_target_pairs={{0,16},{2,18},{4,8},{6,10},{8,12},{10,14},{12,4},{14,6},{16,0},{18... | collective-permute-start | bytes 405512 | tf_op jit(solution)/shard_map/ppermute | solution.py:33
  11.4 2.0 %collective-permute-done.2.refs_3_ = bf16[528,128]{1,0:T(8,128)(2,1)S(1)} collective-permute-done((bf16[528,128]{1,0:T(8,128)(2,1)S(1)}, bf16[528,128]{1,0:T(8,128)(2,1)S(1)}, u32[]{:S(2)}, u32[]{:S(2)}) %collective-permute-start.2) | collective-permute-done | bytes 135200 | tf_op jit(solution)/shard_map/ppermute | solution.py:33
  13.4 1.2 %collective-permute-start.4 = (bf16[528,128]{1,0:T(8,128)(2,1)S(1)}, bf16[528,128]{1,0:T(8,128)(2,1)S(1)}, u32[]{:S(2)}, u32[]{:S(2)}) collective-permute-start(bf16[528,128]{1,0:T(8,128)(2,1)S(1)} %collective-permute-done.2.refs_3_), channel_id=1, source_target_pairs={{0,16},{2,18},{4,8},{6,10},{8,12},{10,14},{12,4},{14,6},{16,0},{18... | collective-permute-start | bytes 405512 | tf_op jit(solution)/shard_map/ppermute | solution.py:33
  14.6 0.0 collective-permute-done.3.refs_4_
  14.6 4.0 %collective-permute-done.4.refs_5_ = bf16[528,128]{1,0:T(8,128)(2,1)S(1)} collective-permute-done((bf16[528,128]{1,0:T(8,128)(2,1)S(1)}, bf16[528,128]{1,0:T(8,128)(2,1)S(1)}, u32[]{:S(2)}, u32[]{:S(2)}) %collective-permute-start.4) | collective-permute-done | bytes 135200 | tf_op jit(solution)/shard_map/ppermute | solution.py:33
  18.6 0.0 copy-done
  18.6 0.0 copy-done.1
  18.6 1.8 %attend_own.1 = (bf16[128,1024]{1,0:T(8,128)(2,1)S(1)}, f32[8,128]{1,0:T(8,128)S(1)}) custom-call(bf16[1,128,2048]{2,1,0:T(8,128)(2,1)S(1)} %copy-done, bf16[1,128,2048]{2,1,0:T(8,128)(2,1)S(1)} %copy-done.1, bf16[528,128]{1,0:T(8,128)(2,1)S(1)} %get-tuple-element.9.refs_0_, bf16[528,128]{1,0:T(8,128)(2,1)S(1)} %collective-permute-done.refs_1_, ...), custom_call_target="tpu_custom_call" | custom-call | flops 3000000000 | tf_op jit(solution)/shard_map/attend_own/pallas_call | solution.py:217
  20.4 1.3 %collective-permute-start.5 = (bf16[128,1024]{1,0:T(8,128)(2,1)S(1)}, bf16[128,1024]{1,0:T(8,128)(2,1)S(1)}, u32[]{:S(2)}, u32[]{:S(2)}) collective-permute-start(bf16[128,1024]{1,0:T(8,128)(2,1)S(1)} %get-tuple-element.11.refs_1_), channel_id=1, source_target_pairs={{0,16},{16,0},{1,17},{17,1},{2,18},{18,2},{3,19},{19,3},{4,20},{20... | collective-permute-start | bytes 786440 | tf_op jit(solution)/shard_map/ppermute | solution.py:33
  21.7 1.3 %collective-permute-done.6.refs_0_ = bf16[2,128,1024]{2,1,0:T(8,128)(2,1)S(1)} collective-permute-done((bf16[2,128,1024]{2,1,0:T(8,128)(2,1)S(1)}, bf16[2,128,1024]{2,1,0:T(8,128)(2,1)S(1)}, u32[]{:S(2)}, u32[]{:S(2)}) %collective-permute-start.6) | collective-permute-done | bytes 524320 | tf_op jit(solution)/shard_map/ppermute | solution.py:33
  23.0 1.8 %attend_part.1 = (bf16[128,1024]{1,0:T(8,128)(2,1)S(1)}, f32[8,128]{1,0:T(8,128)S(1)}) custom-call(bf16[2,128,1024]{2,1,0:T(8,128)(2,1)S(1)} %gate.3.q_ref.s_ref, bf16[2,128,1024]{2,1,0:T(8,128)(2,1)S(1)} %gate.3.q_ref.s_ref, bf16[528,128]{1,0:T(8,128)(2,1)S(1)} %get-tuple-element.9.refs_0_, bf16[528,128]{1,0:T(8,128)(2,1)S(1)} %collective-permute-done.refs_1_, ...), custom_call_target="tpu_custom_call" | custom-call | flops 1000000000 | tf_op jit(solution)/shard_map/attend_part/pallas_call | solution.py:217
  24.7 0.0 copy-start.2
  24.7 2.3 %collective-permute-start.7 = (bf16[128,1024]{1,0:T(8,128)(2,1)S(1)}, bf16[128,1024]{1,0:T(8,128)(2,1)S(1)}, u32[]{:S(2)}, u32[]{:S(2)}) collective-permute-start(bf16[128,1024]{1,0:T(8,128)(2,1)S(1)} %get-tuple-element.13), channel_id=1, source_target_pairs={{0,18},{2,16},{4,22},{6,20},{8,26},{10,24},{12,30},{14,28},{16,2},... | collective-permute-start | bytes 786440 | tf_op jit(solution)/shard_map/ppermute | solution.py:33
  27.1 1.9 %collective-permute-start.8 = (f32[8,128]{1,0:T(8,128)S(1)}, f32[8,128]{1,0:T(8,128)S(1)}, u32[]{:S(2)}, u32[]{:S(2)}) collective-permute-start(f32[8,128]{1,0:T(8,128)S(1)} %get-tuple-element.14), channel_id=1, source_target_pairs={{0,17},{1,16},{16,1},{17,0},{2,19},{3,18},{18,3},{19,2},{4,21},{5,... | collective-permute-start | bytes 12296 | tf_op jit(solution)/shard_map/ppermute | solution.py:33
  28.9 0.0 collective-permute-start.9
  29.0 0.0 copy-done.2
  29.0 5.5 %collective-permute-done.8.sq_a = f32[8,128]{1,0:T(8,128)S(1)} collective-permute-done((f32[8,128]{1,0:T(8,128)S(1)}, f32[8,128]{1,0:T(8,128)S(1)}, u32[]{:S(2)}, u32[]{:S(2)}) %collective-permute-start.8) | collective-permute-done | bytes 4128 | tf_op jit(solution)/shard_map/ppermute | solution.py:33
  34.5 0.0 collective-permute-done.5.own
  34.5 0.0 collective-permute-done.9.sq_b
  34.5 0.0 collective-permute-done.7.part
  34.5 1.3 %norm.1 = (bf16[1,128,2048]{2,1,0:T(8,128)(2,1)}, bf16[1,128,2048]{2,1,0:T(8,128)(2,1)}) custom-call(bf16[128,1024]{1,0:T(8,128)(2,1)S(1)} %collective-permute-done.5.own, bf16[128,1024]{1,0:T(8,128)(2,1)S(1)} %collective-permute-done.7.part, f32[8,128]{1,0:T(8,128)S(1)} %collective-permute-done.8.sq_a, f32[8,128]{1,0:T(8,128)S(1)} %collective-permute-done.9.sq_b, ...), custom_call_target="tpu_custom_call" | custom-call | tf_op jit(solution)/shard_map/norm/pallas_call | solution.py:235
  (3 shorter events, 0.0 us)
Async XLA Ops:
  1.9 5.4 %collective-permute-start = (bf16[528,128]{1,0:T(8,128)(2,1)S(1)}, bf16[528,128]{1,0:T(8,128)(2,1)S(1)}, u32[]{:S(2)}, u32[]{:S(2)}) collective-permute-start(bf16[528,128]{1,0:T(8,128)(2,1)S(1)} %get-tuple-element.10), channel_id=1, source_target_pairs={{0,2},{2,0},{4,6},{6,4},{8,10},{10,8},{12,14},{14,12},{1,3},{3,1},... | collective-permute-start | bytes 405512 | tf_op jit(solution)/shard_map/ppermute | solution.py:33
  4.1 6.1 %collective-permute-start.1 = (bf16[528,128]{1,0:T(8,128)(2,1)S(1)}, bf16[528,128]{1,0:T(8,128)(2,1)S(1)}, u32[]{:S(2)}, u32[]{:S(2)}) collective-permute-start(bf16[528,128]{1,0:T(8,128)(2,1)S(1)} %get-tuple-element.9.refs_0_), channel_id=1, source_target_pairs={{0,4},{2,6},{4,8},{6,10},{8,12},{10,14},{12,0},{14,2},{1,5},{3,7},... | collective-permute-start | bytes 405512 | tf_op jit(solution)/shard_map/ppermute | solution.py:33
  5.4 8.0 %collective-permute-start.2 = (bf16[528,128]{1,0:T(8,128)(2,1)S(1)}, bf16[528,128]{1,0:T(8,128)(2,1)S(1)}, u32[]{:S(2)}, u32[]{:S(2)}) collective-permute-start(bf16[528,128]{1,0:T(8,128)(2,1)S(1)} %get-tuple-element.10), channel_id=1, source_target_pairs={{0,6},{2,4},{4,10},{6,8},{8,14},{10,12},{12,2},{14,0},{1,7},{3,5},... | collective-permute-start | bytes 405512 | tf_op jit(solution)/shard_map/ppermute | solution.py:33
  7.4 11.3 %copy-start = (bf16[1,128,2048]{2,1,0:T(8,128)(2,1)S(1)}, bf16[1,128,2048]{2,1,0:T(8,128)(2,1)}, u32[]{:S(2)}) copy-start(bf16[1,128,2048]{2,1,0:T(8,128)(2,1)} %q_ref.3) | copy-start | bytes 1572868
  7.4 11.3 %copy-start.1 = (bf16[1,128,2048]{2,1,0:T(8,128)(2,1)S(1)}, bf16[1,128,2048]{2,1,0:T(8,128)(2,1)}, u32[]{:S(2)}) copy-start(bf16[1,128,2048]{2,1,0:T(8,128)(2,1)} %s_ref.3) | copy-start | bytes 1572868
  7.4 15.6 %collective-permute-start.6 = (bf16[2,128,1024]{2,1,0:T(8,128)(2,1)S(1)}, bf16[2,128,1024]{2,1,0:T(8,128)(2,1)S(1)}, u32[]{:S(2)}, u32[]{:S(2)}) collective-permute-start(bf16[2,128,1024]{2,1,0:T(8,128)(2,1)S(1)} %gate.2), channel_id=1, source_target_pairs={{0,2},{2,0},{4,6},{6,4},{8,10},{10,8},{12,14},{14,12},{1,3},{3,1},... | collective-permute-start | bytes 1572872 | tf_op jit(solution)/shard_map/ppermute | solution.py:33
  10.1 4.5 %collective-permute-start.3 = (bf16[528,128]{1,0:T(8,128)(2,1)S(1)}, bf16[528,128]{1,0:T(8,128)(2,1)S(1)}, u32[]{:S(2)}, u32[]{:S(2)}) collective-permute-start(bf16[528,128]{1,0:T(8,128)(2,1)S(1)} %collective-permute-done.1.refs_2_), channel_id=1, source_target_pairs={{0,16},{2,18},{4,8},{6,10},{8,12},{10,14},{12,4},{14,6},{16,0},{18... | collective-permute-start | bytes 405512 | tf_op jit(solution)/shard_map/ppermute | solution.py:33
  13.4 5.3 %collective-permute-start.4 = (bf16[528,128]{1,0:T(8,128)(2,1)S(1)}, bf16[528,128]{1,0:T(8,128)(2,1)S(1)}, u32[]{:S(2)}, u32[]{:S(2)}) collective-permute-start(bf16[528,128]{1,0:T(8,128)(2,1)S(1)} %collective-permute-done.2.refs_3_), channel_id=1, source_target_pairs={{0,16},{2,18},{4,8},{6,10},{8,12},{10,14},{12,4},{14,6},{16,0},{18... | collective-permute-start | bytes 405512 | tf_op jit(solution)/shard_map/ppermute | solution.py:33
  20.4 14.1 %collective-permute-start.5 = (bf16[128,1024]{1,0:T(8,128)(2,1)S(1)}, bf16[128,1024]{1,0:T(8,128)(2,1)S(1)}, u32[]{:S(2)}, u32[]{:S(2)}) collective-permute-start(bf16[128,1024]{1,0:T(8,128)(2,1)S(1)} %get-tuple-element.11.refs_1_), channel_id=1, source_target_pairs={{0,16},{16,0},{1,17},{17,1},{2,18},{18,2},{3,19},{19,3},{4,20},{20... | collective-permute-start | bytes 786440 | tf_op jit(solution)/shard_map/ppermute | solution.py:33
  24.7 4.3 %copy-start.2 = (bf16[2048]{0:T(1024)(128)(2,1)S(1)}, bf16[2048]{0:T(1024)(128)(2,1)}, u32[]{:S(2)}) copy-start(bf16[2048]{0:T(1024)(128)(2,1)} %param.11) | copy-start | bytes 12292
  24.7 9.8 %collective-permute-start.7 = (bf16[128,1024]{1,0:T(8,128)(2,1)S(1)}, bf16[128,1024]{1,0:T(8,128)(2,1)S(1)}, u32[]{:S(2)}, u32[]{:S(2)}) collective-permute-start(bf16[128,1024]{1,0:T(8,128)(2,1)S(1)} %get-tuple-element.13), channel_id=1, source_target_pairs={{0,18},{2,16},{4,22},{6,20},{8,26},{10,24},{12,30},{14,28},{16,2},... | collective-permute-start | bytes 786440 | tf_op jit(solution)/shard_map/ppermute | solution.py:33
  27.1 7.5 %collective-permute-start.8 = (f32[8,128]{1,0:T(8,128)S(1)}, f32[8,128]{1,0:T(8,128)S(1)}, u32[]{:S(2)}, u32[]{:S(2)}) collective-permute-start(f32[8,128]{1,0:T(8,128)S(1)} %get-tuple-element.14), channel_id=1, source_target_pairs={{0,17},{1,16},{16,1},{17,0},{2,19},{3,18},{18,3},{19,2},{4,21},{5,... | collective-permute-start | bytes 12296 | tf_op jit(solution)/shard_map/ppermute | solution.py:33
  28.9 5.6 %collective-permute-start.9 = (f32[8,128]{1,0:T(8,128)S(1)}, f32[8,128]{1,0:T(8,128)S(1)}, u32[]{:S(2)}, u32[]{:S(2)}) collective-permute-start(f32[8,128]{1,0:T(8,128)S(1)} %get-tuple-element.15), channel_id=1, source_target_pairs={{0,19},{1,18},{2,17},{3,16},{4,23},{5,22},{6,21},{7,20},{8,27},{9,... | collective-permute-start | bytes 12296 | tf_op jit(solution)/shard_map/ppermute | solution.py:33

commit v3 on v2

v3 whole, which is shorter than its diff:
```python
import functools
import math

import jax
import jax.numpy as jnp
from jax import lax
from jax.experimental import pallas as pl
from jax.experimental.pallas import tpu as pltpu
from jax.sharding import PartitionSpec as P

HEAD = 128
FEATURES = 4096
EPS = 1e-05
SEG_ROWS = 16
NEG = -1e30
VMEM_LIMIT = 40 * 1024 * 1024


def route(x, axes, move):
    sizes = [lax.axis_size(a) for a in axes]
    pairs = []
    for src in range(math.prod(sizes)):
        at, rest = [], src
        for s in reversed(sizes):
            at.insert(0, rest % s)
            rest //= s
        target = move(*at)
        if target is not None:
            to = 0
            for s, v in zip(sizes, target):
                to = to * s + v
            pairs.append((src, to))
    return lax.ppermute(x, tuple(axes) if len(axes) > 1 else axes[0], pairs)


def gate(x, *earlier):
    return pl.pallas_call(
        lambda *refs: None,
        out_shape=jax.ShapeDtypeStruct(x.shape, x.dtype),
        in_specs=[pl.BlockSpec(memory_space=pl.ANY)] * (1 + len(earlier)),
        out_specs=pl.BlockSpec(memory_space=pl.ANY),
        input_output_aliases={0: 0},
        compiler_params=pltpu.CompilerParams(vmem_limit_bytes=VMEM_LIMIT),
        name="gate",
    )(x, *earlier)


def turned(row):
    return jnp.transpose(jnp.broadcast_to(row, (HEAD, HEAD)))


class Fetches:
    def __init__(self, sems):
        self.sems, self.copies = sems, []

    def start(self, src, dst):
        self.copies.append(pltpu.make_async_copy(src, dst, self.sems.at[len(self.copies)]))
        self.copies[-1].start()

    def wait(self):
        for c in self.copies:
            c.wait()


def lanes(start, size):
    return pl.ds(pl.multiple_of(start * HEAD, HEAD), size * HEAD)


def pack_kernel(halves, group, k_ref, v_ref, seg_ref, q_ref, keep, send, far, seg_buf, sems):
    side = lax.axis_index("ctx") % 2
    tiles = halves * group
    fetches = Fetches(sems)
    fetches.start(seg_ref, seg_buf)
    for out, half in ((keep, side), (send, 1 - side)):
        for h in range(halves):
            for n, ref in enumerate((k_ref, v_ref)):
                rows = pl.ds((2 * h + n) * HEAD, HEAD)
                fetches.start(ref.at[0, :, lanes(half * halves + h, 1)], out.at[rows])
    fetches.start(q_ref.at[0, :, lanes((1 - side) * tiles, tiles)], far)
    fetches.wait()
    seg = jnp.broadcast_to(seg_buf[...], (SEG_ROWS, HEAD)).astype(jnp.float32).astype(jnp.bfloat16)
    for out in (keep, send):
        out[2 * halves * HEAD :, :] = seg


def stream_kernel(tiles, s_ref, _, __, out, sems):
    side = lax.axis_index("ctx") % 2
    fetches = Fetches(sems)
    fetches.start(s_ref.at[0, :, lanes((1 - side) * tiles, tiles)], out)
    fetches.wait()


def masks(halves, own, packs, blocks):
    rows = HEAD
    ctx = lax.axis_index("ctx")
    side = ctx % 2
    starts = ctx * rows, (ctx + 1 - 2 * side) * rows
    seg_at = 2 * halves * HEAD

    def seg_of(pack):
        return pack[seg_at : seg_at + SEG_ROWS, :].astype(jnp.float32)[:1]

    lane = lax.broadcasted_iota(jnp.int32, (rows, rows), 1)
    line = lax.broadcasted_iota(jnp.int32, (rows, rows), 0)
    q_seg = turned(seg_of(own[1]))
    tiles = []
    for pack, n in zip(packs, blocks):
        k_start = starts[n % 2] - (n // 2) * 2 * rows
        ok = (lane + k_start <= line + starts[own[0]]) & (lane + k_start >= 0)
        ok &= q_seg == jnp.broadcast_to(seg_of(pack), (rows, rows))
        tiles.append(jnp.where(ok, 0.0, NEG))
    return jnp.concatenate(tiles, axis=1)


def partial_attention(h, group, q, packs, bias, top=None):
    at = 2 * h * HEAD
    keys = jnp.concatenate([p[at : at + HEAD, :] for p in packs], axis=0)
    vals = jnp.concatenate([p[at + HEAD : at + 2 * HEAD, :] for p in packs], axis=0)
    s = lax.dot_general(q, keys, (((1,), (1,)), ((), ())), preferred_element_type=jnp.float32)
    s = s.reshape(group, HEAD, -1) * (HEAD ** (-0.5) * math.log2(math.e)) + bias[None]
    tops = [s[:, :, n * HEAD : (n + 1) * HEAD] for n in range(len(packs))]
    if top is not None:
        tops.append(top)
    new_top = jnp.max(functools.reduce(jnp.maximum, tops), axis=2, keepdims=True)
    w = jnp.exp2(s - new_top)
    total = jnp.sum(w, axis=2, keepdims=True)
    w = w.astype(jnp.bfloat16).reshape(group * HEAD, -1)
    acc = jnp.dot(w, vals, preferred_element_type=jnp.float32).reshape(group, HEAD, HEAD)
    return acc, new_top, total


def own_queries(q_ref, h, halves, group):
    side = lax.axis_index("ctx") % 2
    at = [lanes((side * halves + h) * group + g, 1) for g in range(group)]
    return jnp.concatenate([q_ref[0, :, a] for a in at], axis=0)


def near_kernel(halves, group, blocks, q_ref, *refs):
    *packs, accs, tops, totals = refs
    bias = masks(halves, (0, packs[0]), packs, blocks)
    for h in range(halves):
        q = own_queries(q_ref, h, halves, group)
        acc, top, total = partial_attention(h, group, q, packs, bias)
        accs[h] = acc
        tops[h] = jnp.broadcast_to(top, acc.shape)
        totals[h] = jnp.broadcast_to(total, acc.shape)


def own_kernel(halves, group, blocks, q_ref, s_ref, accs, tops, totals, keep, *refs):
    *packs, out, out_sq = refs
    side = lax.axis_index("ctx") % 2
    bias = masks(halves, (0, keep), packs, blocks)
    sq = jnp.zeros((HEAD, HEAD), jnp.float32)
    for h in range(halves):
        q = own_queries(q_ref, h, halves, group)
        acc, top, total = partial_attention(h, group, q, packs, bias, tops[h])
        scale = jnp.exp2(tops[h] - top)
        acc = accs[h] * scale + acc
        total = totals[h] * scale + total
        att = (acc / total).astype(jnp.bfloat16).astype(jnp.float32)
        for g in range(group):
            n = h * group + g
            stream = s_ref[0, :, lanes(side * halves * group + n, 1)].astype(jnp.float32)
            adv = (stream + att[g]).astype(jnp.bfloat16)
            out[:, n * HEAD : (n + 1) * HEAD] = adv
            sq += adv.astype(jnp.float32) ** 2
    out_sq[...] = row_sums(sq)


def part_kernel(halves, group, q_ref, _, *refs):
    *packs, out = refs
    bias = masks(halves, (1, packs[1]), packs, range(len(packs)))
    for h in range(halves):
        tiles = range(h * group, (h + 1) * group)
        q = jnp.concatenate([q_ref[:, n * HEAD : (n + 1) * HEAD] for n in tiles], axis=0)
        acc, _, total = partial_attention(h, group, q, packs, bias)
        att = (acc / total).astype(jnp.bfloat16)
        for g in range(group):
            n = h * group + g
            out[:, n * HEAD : (n + 1) * HEAD] = att[g]


def add_kernel(tiles, s_ref, att_ref, out, out_sq):
    sq = jnp.zeros((HEAD, HEAD), jnp.float32)
    for n in range(tiles):
        at = slice(n * HEAD, (n + 1) * HEAD)
        adv = s_ref[:, at].astype(jnp.float32) + att_ref[:, at].astype(jnp.float32)
        adv = adv.astype(jnp.bfloat16)
        out[:, at] = adv
        sq += adv.astype(jnp.float32) ** 2
    out_sq[...] = row_sums(sq)


def row_sums(sq):
    return jnp.broadcast_to(jnp.sum(jnp.transpose(sq), axis=0, keepdims=True), (8, HEAD))


def final_kernel(tiles, own, part, sq_a, sq_b, gain_ref, arrived_ref, normed_ref, held, sems):
    side = lax.axis_index("ctx") % 2
    halves = ((side, own), (1 - side, part))
    copies = Fetches(sems)
    for half, p in halves:
        copies.start(p, arrived_ref.at[0, :, lanes(half * tiles, tiles)])
    sq = jnp.zeros((HEAD, HEAD), jnp.float32)
    for p in (own, part):
        for n in range(tiles):
            sq += p[:, n * HEAD : (n + 1) * HEAD].astype(jnp.float32) ** 2
    total = (row_sums(sq) + sq_a[...] + sq_b[...])[:1]
    inv = turned(lax.rsqrt(total / FEATURES + EPS))
    for i, (half, p) in enumerate(halves):
        for n in range(tiles):
            a = p[:, n * HEAD : (n + 1) * HEAD].astype(jnp.float32)
            gain = gain_ref[:, lanes(half * tiles + n, 1)].astype(jnp.float32)
            held[i, :, n * HEAD : (n + 1) * HEAD] = (a * inv * gain).astype(jnp.bfloat16)
        copies.start(held.at[i], normed_ref.at[0, :, lanes(half * tiles, tiles)])
    copies.wait()


def per_device(stream, queries, keys, values, segments, norm_gain):
    rows = stream.shape[1]
    halves = keys.shape[2] // HEAD // 2
    group = queries.shape[2] // keys.shape[2]
    tiles = halves * group
    n_ctx = lax.axis_size("ctx")
    n_pipe = lax.axis_size("pipe")
    level = 2 * rows
    levels_back = (n_ctx * rows // 2 - 1 + level - 1) // level
    vmem = pl.BlockSpec(memory_space=pltpu.VMEM)
    anywhere = pl.BlockSpec(memory_space=pl.ANY)
    params = pltpu.CompilerParams(vmem_limit_bytes=VMEM_LIMIT)
    sums = jax.ShapeDtypeStruct((8, HEAD), jnp.float32)

    def other(c):
        return c + 1 - 2 * (c % 2)

    def up(c):
        return (c + 2) % n_ctx

    def after(p):
        return (p + 1) % n_pipe

    def hop(p, c, distance):
        z, x = c // 2, c % 2
        if z < distance:
            return after(p), c
        return p, 2 * (z + 1 if 2 * z + 2 < n_ctx else distance) + x

    def buffer(*shape):
        return jax.ShapeDtypeStruct(shape, jnp.bfloat16)

    def held(x):
        return pltpu.with_memory_space_constraint(x, pltpu.HBM)

    def kernel(body, name, shapes, specs, *args, scratch=(), flops=0):
        return pl.pallas_call(
            body,
            out_shape=shapes,
            in_specs=specs,
            out_specs=[vmem] * len(shapes),
            scratch_shapes=scratch,
            compiler_params=params,
            cost_estimate=pl.CostEstimate(flops=flops, bytes_accessed=0, transcendentals=0),
            name=name,
        )(*args)

    kv_rows = 2 * halves * HEAD + SEG_ROWS
    keep, send, far_q = kernel(
        functools.partial(pack_kernel, halves, group),
        "pack",
        [buffer(kv_rows, HEAD)] * 2 + [buffer(rows, tiles * HEAD)],
        [anywhere] * 4,
        *(held(x) for x in (keys, values, segments, queries)),
        scratch=[pltpu.VMEM((1, rows), jnp.int32), pltpu.SemaphoreType.DMA((2 + 4 * halves,))],
    )
    packs = [
        keep,
        route(send, ["ctx"], lambda c: (other(c),)),
        route(keep, ["ctx"], lambda c: (up(c),)),
        route(send, ["ctx"], lambda c: (up(other(c)),)),
    ]
    far_q = route(gate(far_q, packs[1]), ["ctx"], lambda c: (other(c),))
    for n in range(1, levels_back):
        packs += [route(b, ["pipe", "ctx"], lambda p, c: hop(p, c, n)) for b in packs[-2:]]
    (far,) = kernel(
        functools.partial(stream_kernel, tiles),
        "stream",
        [buffer(rows, tiles * HEAD)],
        [anywhere] * 3,
        held(stream),
        packs[2],
        packs[3],
        scratch=[pltpu.SemaphoreType.DMA((1,))],
    )
    far = route(far, ["ctx"], lambda c: (other(c),))

    near, late = [0, 2, 3], [1, *range(4, len(packs))]
    state = [jax.ShapeDtypeStruct((halves, group, rows, HEAD), jnp.float32)] * 3
    state = kernel(
        functools.partial(near_kernel, halves, group, near),
        "attend_near",
        state,
        [vmem] * (1 + len(near)),
        queries,
        *(packs[n] for n in near),
        flops=1000000000,
    )
    own, own_sq = kernel(
        functools.partial(own_kernel, halves, group, late),
        "attend_own",
        [buffer(rows, tiles * HEAD), sums],
        [vmem] * (6 + len(late)),
        queries,
        stream,
        *state,
        keep,
        *(packs[n] for n in late),
        flops=1000000000,
    )
    straight = route(own, ["pipe"], lambda p: (after(p),))
    sq_a = route(own_sq, ["pipe", "tp"], lambda p, t: (after(p), 1 - t))
    (att,) = kernel(
        functools.partial(part_kernel, halves, group),
        "attend_part",
        [buffer(rows, tiles * HEAD)],
        [vmem, anywhere] + [vmem] * len(packs),
        far_q,
        own,
        *packs,
        flops=1000000000,
    )
    part, part_sq = kernel(
        functools.partial(add_kernel, tiles), "add", [buffer(rows, tiles * HEAD), sums], [vmem] * 2, far, att
    )
    across = route(part, ["pipe", "ctx"], lambda p, c: (after(p), other(c)))
    sq_b = route(part_sq, ["pipe", "ctx", "tp"], lambda p, c, t: (after(p), other(c), 1 - t))
    return tuple(
        pl.pallas_call(
            functools.partial(final_kernel, tiles),
            out_shape=[buffer(*stream.shape)] * 2,
            in_specs=[vmem] * 5,
            out_specs=[anywhere] * 2,
            scratch_shapes=[pltpu.VMEM((2, rows, tiles * HEAD), jnp.bfloat16), pltpu.SemaphoreType.DMA((4,))],
            compiler_params=params,
            name="norm",
        )(straight, across, sq_a, sq_b, norm_gain[None])
    )


def solution(mesh):
    spec = P("pipe", "ctx", "tp")
    return jax.shard_map(
        per_device,
        mesh=mesh,
        in_specs=(spec, spec, spec, spec, P("pipe", "ctx"), P("tp")),
        out_specs=(spec, spec),
        check_vma=False,
    )
```

time: 36.4 us -> 35.6 us (0.978)
  waiting for transfers between devices: 15.2 us -> 11.2 us
  starting transfers between devices: 13.8 us -> 15.8 us
  Pallas kernels: 6.18 us -> 7.34 us
    ppermute x10 -> x11, waiting for transfers between devices: 15.2 us -> 11.2 us  [route(): return lax.ppermute(x, tuple(axes) if len(axes) > 1 else axes[0], pairs)]
    ppermute x10 -> x11, starting transfers between devices: 13.8 us -> 15.8 us  [route(): return lax.ppermute(x, tuple(axes) if len(axes) > 1 else axes[0], pairs)]
    pallas_call x3 -> x6, Pallas kernels: 4.84 us -> 6.1 us  [kernel(): pl.pallas_call(body, out_shape=shapes, in_specs=specs, out_specs=[vmem] *...]
  transfers between devices with their start and end apart: 10 -> 11, of which waited for: 6 -> 5; matrix products, arithmetic and copies ran while one was open for 0% -> 0% of each run, Pallas kernels for 10% -> 14%
where the time goes in v3:
time: 35.6 us; the launch traced here: 35.1 us
  starting transfers between devices  15.8 us (44%)
  waiting for transfers between devices  11.2 us (31%)
  Pallas kernels  7.34 us (21%)
  between operations  0.72 us (2%)
    ppermute x11, starting transfers between devices, route(): return lax.ppermute(x, tuple(axes) if len(axes) > 1 else axes[0], pairs)  15.8 us
    ppermute x11, waiting for transfers between devices, route(): return lax.ppermute(x, tuple(axes) if len(axes) > 1 else axes[0], pairs)  11.2 us
    pallas_call x6, Pallas kernels, kernel(): pl.pallas_call(body, out_shape=shapes, in_specs=specs, out_specs=[vmem] *...  6.1 us
    pallas_call x1, Pallas kernels, per_device(): pl.pallas_call(functools.partial(final_kernel, tiles), out_shape=[buffer(...  1.23 us
  transfers between devices with their start and end apart: 11, of which 5 were waited for; matrix products, arithmetic and copies ran while one was open for 0% of the time, Pallas kernels for 14%

profile of v3, /device:TPU:1, one launch (start us, length us, event | category | flops | bytes accessed | tf_op | source)
XLA Modules:
  0.0 35.1 jit_solution(16761336759106187097)
XLA Ops:
  0.6 1.2 %pack.1 = (bf16[528,128]{1,0:T(8,128)(2,1)S(1)}, bf16[528,128]{1,0:T(8,128)(2,1)S(1)}, bf16[128,1024]{1,0:T(8,128)(2,1)S(1)}) custom-call(bf16[1,128,512]{2,1,0:T(8,128)(2,1)} %k_ref.1, bf16[1,128,512]{2,1,0:T(8,128)(2,1)} %v_ref.1, s32[1,128]{1,0:T(1,128)} %seg_ref.1, bf16[1,128,2048]{2,1,0:T(8,128)(2,1)} %q_ref.5), custom_call_target="tpu_custom_call" | custom-call | tf_op jit(solution)/shard_map/pack/pallas_call | solution.py:255
  1.9 2.1 %collective-permute-start.2 = (bf16[528,128]{1,0:T(8,128)(2,1)S(1)}, bf16[528,128]{1,0:T(8,128)(2,1)S(1)}, u32[]{:S(2)}, u32[]{:S(2)}) collective-permute-start(bf16[528,128]{1,0:T(8,128)(2,1)S(1)} %get-tuple-element.13), channel_id=1, source_target_pairs={{0,2},{2,0},{4,6},{6,4},{8,10},{10,8},{12,14},{14,12},{1,3},{3,1},... | collective-permute-start | bytes 405512 | tf_op jit(solution)/shard_map/ppermute | solution.py:33
  4.0 1.3 %collective-permute-start = (bf16[528,128]{1,0:T(8,128)(2,1)S(1)}, bf16[528,128]{1,0:T(8,128)(2,1)S(1)}, u32[]{:S(2)}, u32[]{:S(2)}) collective-permute-start(bf16[528,128]{1,0:T(8,128)(2,1)S(1)} %get-tuple-element.12.refs_0_.keep), channel_id=1, source_target_pairs={{0,4},{2,6},{4,8},{6,10},{8,12},{10,14},{12,0},{14,2},{1,5},{3,7},... | collective-permute-start | bytes 405512 | tf_op jit(solution)/shard_map/ppermute | solution.py:33
  5.3 1.3 %collective-permute-start.1 = (bf16[528,128]{1,0:T(8,128)(2,1)S(1)}, bf16[528,128]{1,0:T(8,128)(2,1)S(1)}, u32[]{:S(2)}, u32[]{:S(2)}) collective-permute-start(bf16[528,128]{1,0:T(8,128)(2,1)S(1)} %get-tuple-element.13), channel_id=1, source_target_pairs={{0,6},{2,4},{4,10},{6,8},{8,14},{10,12},{12,2},{14,0},{1,7},{3,5},... | collective-permute-start | bytes 405512 | tf_op jit(solution)/shard_map/ppermute | solution.py:33
  6.5 0.7 %collective-permute-done.2.refs_0_.refs_1_ = bf16[528,128]{1,0:T(8,128)(2,1)S(1)} collective-permute-done((bf16[528,128]{1,0:T(8,128)(2,1)S(1)}, bf16[528,128]{1,0:T(8,128)(2,1)S(1)}, u32[]{:S(2)}, u32[]{:S(2)}) %collective-permute-start.2) | collective-permute-done | bytes 135200 | tf_op jit(solution)/shard_map/ppermute | solution.py:33
  7.3 1.1 %collective-permute-start.7 = (bf16[128,1024]{1,0:T(8,128)(2,1)S(1)}, bf16[128,1024]{1,0:T(8,128)(2,1)S(1)}, u32[]{:S(2)}, u32[]{:S(2)}) collective-permute-start(bf16[128,1024]{1,0:T(8,128)(2,1)S(1)} %gate.1), channel_id=1, source_target_pairs={{0,2},{2,0},{4,6},{6,4},{8,10},{10,8},{12,14},{14,12},{1,3},{3,1},... | collective-permute-start | bytes 786440 | tf_op jit(solution)/shard_map/ppermute | solution.py:33
  8.4 1.6 %collective-permute-done.refs_1_._.refs_2_ = bf16[528,128]{1,0:T(8,128)(2,1)S(1)} collective-permute-done((bf16[528,128]{1,0:T(8,128)(2,1)S(1)}, bf16[528,128]{1,0:T(8,128)(2,1)S(1)}, u32[]{:S(2)}, u32[]{:S(2)}) %collective-permute-start) | collective-permute-done | bytes 135200 | tf_op jit(solution)/shard_map/ppermute | solution.py:33
  10.0 1.2 %collective-permute-start.3 = (bf16[528,128]{1,0:T(8,128)(2,1)S(1)}, bf16[528,128]{1,0:T(8,128)(2,1)S(1)}, u32[]{:S(2)}, u32[]{:S(2)}) collective-permute-start(bf16[528,128]{1,0:T(8,128)(2,1)S(1)} %collective-permute-done.refs_1_._.refs_2_), channel_id=1, source_target_pairs={{0,16},{2,18},{4,8},{6,10},{8,12},{10,14},{12,4},{14,6},{16,0},{18... | collective-permute-start | bytes 405512 | tf_op jit(solution)/shard_map/ppermute | solution.py:33
  11.3 2.0 %collective-permute-done.1.refs_2_.__.refs_3_ = bf16[528,128]{1,0:T(8,128)(2,1)S(1)} collective-permute-done((bf16[528,128]{1,0:T(8,128)(2,1)S(1)}, bf16[528,128]{1,0:T(8,128)(2,1)S(1)}, u32[]{:S(2)}, u32[]{:S(2)}) %collective-permute-start.1) | collective-permute-done | bytes 135200 | tf_op jit(solution)/shard_map/ppermute | solution.py:33
  13.3 1.2 %collective-permute-start.4 = (bf16[528,128]{1,0:T(8,128)(2,1)S(1)}, bf16[528,128]{1,0:T(8,128)(2,1)S(1)}, u32[]{:S(2)}, u32[]{:S(2)}) collective-permute-start(bf16[528,128]{1,0:T(8,128)(2,1)S(1)} %collective-permute-done.1.refs_2_.__.refs_3_), channel_id=1, source_target_pairs={{0,16},{2,18},{4,8},{6,10},{8,12},{10,14},{12,4},{14,6},{16,0},{18... | collective-permute-start | bytes 405512 | tf_op jit(solution)/shard_map/ppermute | solution.py:33
  14.5 1.0 %stream.1 = bf16[128,1024]{1,0:T(8,128)(2,1)S(1)} custom-call(bf16[1,128,2048]{2,1,0:T(8,128)(2,1)} %s_ref.3, bf16[528,128]{1,0:T(8,128)(2,1)S(1)} %collective-permute-done.refs_1_._.refs_2_, bf16[528,128]{1,0:T(8,128)(2,1)S(1)} %collective-permute-done.1.refs_2_.__.refs_3_), custom_call_target="tpu_custom_call" | custom-call | tf_op jit(solution)/shard_map/stream/pallas_call | solution.py:255
  15.5 0.0 copy-start.1
  15.5 0.9 %collective-permute-start.6 = (bf16[128,1024]{1,0:T(8,128)(2,1)S(1)}, bf16[128,1024]{1,0:T(8,128)(2,1)S(1)}, u32[]{:S(2)}, u32[]{:S(2)}) collective-permute-start(bf16[128,1024]{1,0:T(8,128)(2,1)S(1)} %stream.1), channel_id=1, source_target_pairs={{0,2},{2,0},{4,6},{6,4},{8,10},{10,8},{12,14},{14,12},{1,3},{3,1},... | collective-permute-start | bytes 786440 | tf_op jit(solution)/shard_map/ppermute | solution.py:33
  16.4 0.0 copy-done
  16.4 0.9 %attend_near.1 = (f32[2,4,128,128]{3,2,1,0:T(8,128)S(1)}, f32[2,4,128,128]{3,2,1,0:T(8,128)S(1)}, f32[2,4,128,128]{3,2,1,0:T(8,128)S(1)}) custom-call(bf16[1,128,2048]{2,1,0:T(8,128)(2,1)S(1)} %copy-done, bf16[528,128]{1,0:T(8,128)(2,1)S(1)} %get-tuple-element.12.refs_0_.keep, bf16[528,128]{1,0:T(8,128)(2,1)S(1)} %collective-permute-done.refs_1_._.refs_2_, ...), custom_call_target="tpu_custom_call" | custom-call | flops 1000000000 | tf_op jit(solution)/shard_map/attend_near/pallas_call | solution.py:255
  17.3 0.0 collective-permute-done.3.refs_1_.refs_4_
  17.3 1.2 %collective-permute-done.4.refs_2_.refs_5_ = bf16[528,128]{1,0:T(8,128)(2,1)S(1)} collective-permute-done((bf16[528,128]{1,0:T(8,128)(2,1)S(1)}, bf16[528,128]{1,0:T(8,128)(2,1)S(1)}, u32[]{:S(2)}, u32[]{:S(2)}) %collective-permute-start.4) | collective-permute-done | bytes 135200 | tf_op jit(solution)/shard_map/ppermute | solution.py:33
  18.5 1.2 %attend_own.1 = (bf16[128,1024]{1,0:T(8,128)(2,1)S(1)}, f32[8,128]{1,0:T(8,128)S(1)}) custom-call(bf16[1,128,2048]{2,1,0:T(8,128)(2,1)S(1)} %copy-done, bf16[1,128,2048]{2,1,0:T(8,128)(2,1)S(1)} %copy-done.1, f32[2,4,128,128]{3,2,1,0:T(8,128)S(1)} %get-tuple-element.14.accs, f32[2,4,128,128]{3,2,1,0:T(8,128)S(1)} %get-tuple-element.15.tops, ...), custom_call_target="tpu_custom_call" | custom-call | flops 1000000000 | tf_op jit(solution)/shard_map/attend_own/pallas_call | solution.py:255
  19.7 1.3 %collective-permute-start.5 = (bf16[128,1024]{1,0:T(8,128)(2,1)S(1)}, bf16[128,1024]{1,0:T(8,128)(2,1)S(1)}, u32[]{:S(2)}, u32[]{:S(2)}) collective-permute-start(bf16[128,1024]{1,0:T(8,128)(2,1)S(1)} %get-tuple-element.17._), channel_id=1, source_target_pairs={{0,16},{16,0},{1,17},{17,1},{2,18},{18,2},{3,19},{19,3},{4,20},{20... | collective-permute-start | bytes 786440 | tf_op jit(solution)/shard_map/ppermute | solution.py:33
  21.0 0.0 collective-permute-done.7.q_ref
  21.0 1.7 %attend_part.1.att_ref = bf16[128,1024]{1,0:T(8,128)(2,1)S(1)} custom-call(bf16[128,1024]{1,0:T(8,128)(2,1)S(1)} %collective-permute-done.7.q_ref, bf16[128,1024]{1,0:T(8,128)(2,1)S(1)} %get-tuple-element.17._, bf16[528,128]{1,0:T(8,128)(2,1)S(1)} %get-tuple-element.12.refs_0_.keep, bf16[528,128]{1,0:T(8,128)(2,1)S(1)} %collective-permute-done.2.refs_0_.refs_1_, ...), custom_call_target="tpu_custom_call" | custom-call | flops 1000000000 | tf_op jit(solution)/shard_map/attend_part/pallas_call | solution.py:255
  22.7 0.0 collective-permute-done.6.s_ref
  22.7 0.2 add.1
  22.9 0.0 copy-start.2
  22.9 1.3 %collective-permute-start.8 = (bf16[128,1024]{1,0:T(8,128)(2,1)S(1)}, bf16[128,1024]{1,0:T(8,128)(2,1)S(1)}, u32[]{:S(2)}, u32[]{:S(2)}) collective-permute-start(bf16[128,1024]{1,0:T(8,128)(2,1)S(1)} %get-tuple-element.19), channel_id=1, source_target_pairs={{0,18},{2,16},{4,22},{6,20},{8,26},{10,24},{12,30},{14,28},{16,2},... | collective-permute-start | bytes 786440 | tf_op jit(solution)/shard_map/ppermute | solution.py:33
  24.2 4.0 %collective-permute-start.9 = (f32[8,128]{1,0:T(8,128)S(1)}, f32[8,128]{1,0:T(8,128)S(1)}, u32[]{:S(2)}, u32[]{:S(2)}) collective-permute-start(f32[8,128]{1,0:T(8,128)S(1)} %get-tuple-element.20), channel_id=1, source_target_pairs={{0,17},{1,16},{16,1},{17,0},{2,19},{3,18},{18,3},{19,2},{4,21},{5,... | collective-permute-start | bytes 12296 | tf_op jit(solution)/shard_map/ppermute | solution.py:33
  28.2 0.0 collective-permute-start.10
  28.2 5.6 %collective-permute-done.9.sq_a = f32[8,128]{1,0:T(8,128)S(1)} collective-permute-done((f32[8,128]{1,0:T(8,128)S(1)}, f32[8,128]{1,0:T(8,128)S(1)}, u32[]{:S(2)}, u32[]{:S(2)}) %collective-permute-start.9) | collective-permute-done | bytes 4128 | tf_op jit(solution)/shard_map/ppermute | solution.py:33
  33.9 0.0 collective-permute-done.10.sq_b
  33.9 0.0 collective-permute-done.5.own
  33.9 0.0 collective-permute-done.8.part
  33.9 1.2 %norm.1 = (bf16[1,128,2048]{2,1,0:T(8,128)(2,1)}, bf16[1,128,2048]{2,1,0:T(8,128)(2,1)}) custom-call(bf16[128,1024]{1,0:T(8,128)(2,1)S(1)} %collective-permute-done.5.own, bf16[128,1024]{1,0:T(8,128)(2,1)S(1)} %collective-permute-done.8.part, f32[8,128]{1,0:T(8,128)S(1)} %collective-permute-done.9.sq_a, f32[8,128]{1,0:T(8,128)S(1)} %collective-permute-done.10.sq_b, ...), custom_call_target="tpu_custom_call" | custom-call | tf_op jit(solution)/shard_map/norm/pallas_call | solution.py:337
  (5 shorter events, 0.0 us)
Async XLA Ops:
  1.9 5.4 %collective-permute-start.2 = (bf16[528,128]{1,0:T(8,128)(2,1)S(1)}, bf16[528,128]{1,0:T(8,128)(2,1)S(1)}, u32[]{:S(2)}, u32[]{:S(2)}) collective-permute-start(bf16[528,128]{1,0:T(8,128)(2,1)S(1)} %get-tuple-element.13), channel_id=1, source_target_pairs={{0,2},{2,0},{4,6},{6,4},{8,10},{10,8},{12,14},{14,12},{1,3},{3,1},... | collective-permute-start | bytes 405512 | tf_op jit(solution)/shard_map/ppermute | solution.py:33
  4.0 6.1 %collective-permute-start = (bf16[528,128]{1,0:T(8,128)(2,1)S(1)}, bf16[528,128]{1,0:T(8,128)(2,1)S(1)}, u32[]{:S(2)}, u32[]{:S(2)}) collective-permute-start(bf16[528,128]{1,0:T(8,128)(2,1)S(1)} %get-tuple-element.12.refs_0_.keep), channel_id=1, source_target_pairs={{0,4},{2,6},{4,8},{6,10},{8,12},{10,14},{12,0},{14,2},{1,5},{3,7},... | collective-permute-start | bytes 405512 | tf_op jit(solution)/shard_map/ppermute | solution.py:33
  5.3 8.0 %collective-permute-start.1 = (bf16[528,128]{1,0:T(8,128)(2,1)S(1)}, bf16[528,128]{1,0:T(8,128)(2,1)S(1)}, u32[]{:S(2)}, u32[]{:S(2)}) collective-permute-start(bf16[528,128]{1,0:T(8,128)(2,1)S(1)} %get-tuple-element.13), channel_id=1, source_target_pairs={{0,6},{2,4},{4,10},{6,8},{8,14},{10,12},{12,2},{14,0},{1,7},{3,5},... | collective-permute-start | bytes 405512 | tf_op jit(solution)/shard_map/ppermute | solution.py:33
  7.3 9.1 %copy-start = (bf16[1,128,2048]{2,1,0:T(8,128)(2,1)S(1)}, bf16[1,128,2048]{2,1,0:T(8,128)(2,1)}, u32[]{:S(2)}) copy-start(bf16[1,128,2048]{2,1,0:T(8,128)(2,1)} %q_ref.5) | copy-start | bytes 1572868
  7.3 13.7 %collective-permute-start.7 = (bf16[128,1024]{1,0:T(8,128)(2,1)S(1)}, bf16[128,1024]{1,0:T(8,128)(2,1)S(1)}, u32[]{:S(2)}, u32[]{:S(2)}) collective-permute-start(bf16[128,1024]{1,0:T(8,128)(2,1)S(1)} %gate.1), channel_id=1, source_target_pairs={{0,2},{2,0},{4,6},{6,4},{8,10},{10,8},{12,14},{14,12},{1,3},{3,1},... | collective-permute-start | bytes 786440 | tf_op jit(solution)/shard_map/ppermute | solution.py:33
  10.0 7.3 %collective-permute-start.3 = (bf16[528,128]{1,0:T(8,128)(2,1)S(1)}, bf16[528,128]{1,0:T(8,128)(2,1)S(1)}, u32[]{:S(2)}, u32[]{:S(2)}) collective-permute-start(bf16[528,128]{1,0:T(8,128)(2,1)S(1)} %collective-permute-done.refs_1_._.refs_2_), channel_id=1, source_target_pairs={{0,16},{2,18},{4,8},{6,10},{8,12},{10,14},{12,4},{14,6},{16,0},{18... | collective-permute-start | bytes 405512 | tf_op jit(solution)/shard_map/ppermute | solution.py:33
  13.3 5.3 %collective-permute-start.4 = (bf16[528,128]{1,0:T(8,128)(2,1)S(1)}, bf16[528,128]{1,0:T(8,128)(2,1)S(1)}, u32[]{:S(2)}, u32[]{:S(2)}) collective-permute-start(bf16[528,128]{1,0:T(8,128)(2,1)S(1)} %collective-permute-done.1.refs_2_.__.refs_3_), channel_id=1, source_target_pairs={{0,16},{2,18},{4,8},{6,10},{8,12},{10,14},{12,4},{14,6},{16,0},{18... | collective-permute-start | bytes 405512 | tf_op jit(solution)/shard_map/ppermute | solution.py:33
  15.5 3.1 %copy-start.1 = (bf16[1,128,2048]{2,1,0:T(8,128)(2,1)S(1)}, bf16[1,128,2048]{2,1,0:T(8,128)(2,1)}, u32[]{:S(2)}) copy-start(bf16[1,128,2048]{2,1,0:T(8,128)(2,1)} %s_ref.3) | copy-start | bytes 1572868
  15.5 7.2 %collective-permute-start.6 = (bf16[128,1024]{1,0:T(8,128)(2,1)S(1)}, bf16[128,1024]{1,0:T(8,128)(2,1)S(1)}, u32[]{:S(2)}, u32[]{:S(2)}) collective-permute-start(bf16[128,1024]{1,0:T(8,128)(2,1)S(1)} %stream.1), channel_id=1, source_target_pairs={{0,2},{2,0},{4,6},{6,4},{8,10},{10,8},{12,14},{14,12},{1,3},{3,1},... | collective-permute-start | bytes 786440 | tf_op jit(solution)/shard_map/ppermute | solution.py:33
  19.7 14.2 %collective-permute-start.5 = (bf16[128,1024]{1,0:T(8,128)(2,1)S(1)}, bf16[128,1024]{1,0:T(8,128)(2,1)S(1)}, u32[]{:S(2)}, u32[]{:S(2)}) collective-permute-start(bf16[128,1024]{1,0:T(8,128)(2,1)S(1)} %get-tuple-element.17._), channel_id=1, source_target_pairs={{0,16},{16,0},{1,17},{17,1},{2,18},{18,2},{3,19},{19,3},{4,20},{20... | collective-permute-start | bytes 786440 | tf_op jit(solution)/shard_map/ppermute | solution.py:33
  22.9 5.3 %copy-start.2 = (bf16[2048]{0:T(1024)(128)(2,1)S(1)}, bf16[2048]{0:T(1024)(128)(2,1)}, u32[]{:S(2)}) copy-start(bf16[2048]{0:T(1024)(128)(2,1)} %param.11) | copy-start | bytes 12292
  22.9 11.0 %collective-permute-start.8 = (bf16[128,1024]{1,0:T(8,128)(2,1)S(1)}, bf16[128,1024]{1,0:T(8,128)(2,1)S(1)}, u32[]{:S(2)}, u32[]{:S(2)}) collective-permute-start(bf16[128,1024]{1,0:T(8,128)(2,1)S(1)} %get-tuple-element.19), channel_id=1, source_target_pairs={{0,18},{2,16},{4,22},{6,20},{8,26},{10,24},{12,30},{14,28},{16,2},... | collective-permute-start | bytes 786440 | tf_op jit(solution)/shard_map/ppermute | solution.py:33
  24.2 9.6 %collective-permute-start.9 = (f32[8,128]{1,0:T(8,128)S(1)}, f32[8,128]{1,0:T(8,128)S(1)}, u32[]{:S(2)}, u32[]{:S(2)}) collective-permute-start(f32[8,128]{1,0:T(8,128)S(1)} %get-tuple-element.20), channel_id=1, source_target_pairs={{0,17},{1,16},{16,1},{17,0},{2,19},{3,18},{18,3},{19,2},{4,21},{5,... | collective-permute-start | bytes 12296 | tf_op jit(solution)/shard_map/ppermute | solution.py:33
  28.2 5.7 %collective-permute-start.10 = (f32[8,128]{1,0:T(8,128)S(1)}, f32[8,128]{1,0:T(8,128)S(1)}, u32[]{:S(2)}, u32[]{:S(2)}) collective-permute-start(f32[8,128]{1,0:T(8,128)S(1)} %get-tuple-element.21), channel_id=1, source_target_pairs={{0,19},{1,18},{2,17},{3,16},{4,23},{5,22},{6,21},{7,20},{8,27},{9,... | collective-permute-start | bytes 12296 | tf_op jit(solution)/shard_map/ppermute | solution.py:33

commit v4 on v3

--- a/solution.py
+++ b/solution.py
@@ -66,7 +66,7 @@
     return pl.ds(pl.multiple_of(start * HEAD, HEAD), size * HEAD)
 
 
-def pack_kernel(halves, group, k_ref, v_ref, seg_ref, q_ref, keep, send, far, seg_buf, sems):
+def pack_kernel(halves, group, k_ref, v_ref, seg_ref, q_ref, s_ref, keep, send, far_q, far_s, seg_buf, sems):
     side = lax.axis_index("ctx") % 2
     tiles = halves * group
     fetches = Fetches(sems)
@@ -76,18 +76,12 @@
             for n, ref in enumerate((k_ref, v_ref)):
                 rows = pl.ds((2 * h + n) * HEAD, HEAD)
                 fetches.start(ref.at[0, :, lanes(half * halves + h, 1)], out.at[rows])
-    fetches.start(q_ref.at[0, :, lanes((1 - side) * tiles, tiles)], far)
+    for ref, far in ((q_ref, far_q), (s_ref, far_s)):
+        fetches.start(ref.at[0, :, lanes((1 - side) * tiles, tiles)], far)
     fetches.wait()
     seg = jnp.broadcast_to(seg_buf[...], (SEG_ROWS, HEAD)).astype(jnp.float32).astype(jnp.bfloat16)
     for out in (keep, send):
         out[2 * halves * HEAD :, :] = seg
-
-
-def stream_kernel(tiles, s_ref, _, __, out, sems):
-    side = lax.axis_index("ctx") % 2
-    fetches = Fetches(sems)
-    fetches.start(s_ref.at[0, :, lanes((1 - side) * tiles, tiles)], out)
-    fetches.wait()
 
 
 def masks(halves, own, packs, blocks):
@@ -146,38 +140,58 @@
         totals[h] = jnp.broadcast_to(total, acc.shape)
 
 
+def has_late(blocks):
+    return lax.axis_index("ctx") // 2 >= blocks[0] // 2
+
+
 def own_kernel(halves, group, blocks, q_ref, s_ref, accs, tops, totals, keep, *refs):
     *packs, out, out_sq = refs
     side = lax.axis_index("ctx") % 2
-    bias = masks(halves, (0, keep), packs, blocks)
-    sq = jnp.zeros((HEAD, HEAD), jnp.float32)
-    for h in range(halves):
-        q = own_queries(q_ref, h, halves, group)
-        acc, top, total = partial_attention(h, group, q, packs, bias, tops[h])
-        scale = jnp.exp2(tops[h] - top)
-        acc = accs[h] * scale + acc
-        total = totals[h] * scale + total
-        att = (acc / total).astype(jnp.bfloat16).astype(jnp.float32)
-        for g in range(group):
-            n = h * group + g
-            stream = s_ref[0, :, lanes(side * halves * group + n, 1)].astype(jnp.float32)
-            adv = (stream + att[g]).astype(jnp.bfloat16)
-            out[:, n * HEAD : (n + 1) * HEAD] = adv
-            sq += adv.astype(jnp.float32) ** 2
-    out_sq[...] = row_sums(sq)
-
-
-def part_kernel(halves, group, q_ref, _, *refs):
+
+    def finish(results):
+        sq = jnp.zeros((HEAD, HEAD), jnp.float32)
+        for h, (acc, total) in enumerate(results):
+            att = (acc / total).astype(jnp.bfloat16).astype(jnp.float32)
+            for g in range(group):
+                n = h * group + g
+                stream = s_ref[0, :, lanes(side * halves * group + n, 1)].astype(jnp.float32)
+                adv = (stream + att[g]).astype(jnp.bfloat16)
+                out[:, n * HEAD : (n + 1) * HEAD] = adv
+                sq += adv.astype(jnp.float32) ** 2
+        out_sq[...] = row_sums(sq)
+
+    @pl.when(has_late(blocks))
+    def _():
+        bias = masks(halves, (0, keep), packs, blocks)
+        results = []
+        for h in range(halves):
+            q = own_queries(q_ref, h, halves, group)
+            acc, top, total = partial_attention(h, group, q, packs, bias, tops[h])
+            scale = jnp.exp2(tops[h] - top)
+            results.append((accs[h] * scale + acc, totals[h] * scale + total))
+        finish(results)
+
+    @pl.when(jnp.logical_not(has_late(blocks)))
+    def _():
+        finish([(accs[h], totals[h]) for h in range(halves)])
+
+
+def part_kernel(halves, group, blocks, q_ref, _, *refs):
     *packs, out = refs
-    bias = masks(halves, (1, packs[1]), packs, range(len(packs)))
-    for h in range(halves):
-        tiles = range(h * group, (h + 1) * group)
-        q = jnp.concatenate([q_ref[:, n * HEAD : (n + 1) * HEAD] for n in tiles], axis=0)
-        acc, _, total = partial_attention(h, group, q, packs, bias)
-        att = (acc / total).astype(jnp.bfloat16)
-        for g in range(group):
-            n = h * group + g
-            out[:, n * HEAD : (n + 1) * HEAD] = att[g]
+
+    def attend(packs):
+        bias = masks(halves, (1, packs[1]), packs, range(len(packs)))
+        for h in range(halves):
+            tiles = range(h * group, (h + 1) * group)
+            q = jnp.concatenate([q_ref[:, n * HEAD : (n + 1) * HEAD] for n in tiles], axis=0)
+            acc, _, total = partial_attention(h, group, q, packs, bias)
+            att = (acc / total).astype(jnp.bfloat16)
+            for g in range(group):
+                n = h * group + g
+                out[:, n * HEAD : (n + 1) * HEAD] = att[g]
+
+    pl.when(has_late(blocks))(lambda: attend(packs))
+    pl.when(jnp.logical_not(has_late(blocks)))(lambda: attend(packs[: blocks[0]]))
 
 
 def add_kernel(tiles, s_ref, att_ref, out, out_sq):
@@ -239,11 +253,11 @@
     def after(p):
         return (p + 1) % n_pipe
 
-    def hop(p, c, distance):
+    def hop(c, t, distance):
         z, x = c // 2, c % 2
         if z < distance:
-            return after(p), c
-        return p, 2 * (z + 1 if 2 * z + 2 < n_ctx else distance) + x
+            return c, 1 - t
+        return 2 * (z + 1 if 2 * z + 2 < n_ctx else distance) + x, t
 
     def buffer(*shape):
         return jax.ShapeDtypeStruct(shape, jnp.bfloat16)
@@ -264,13 +278,13 @@
         )(*args)
 
     kv_rows = 2 * halves * HEAD + SEG_ROWS
-    keep, send, far_q = kernel(
+    keep, send, far_q, far_s = kernel(
         functools.partial(pack_kernel, halves, group),
         "pack",
-        [buffer(kv_rows, HEAD)] * 2 + [buffer(rows, tiles * HEAD)],
-        [anywhere] * 4,
-        *(held(x) for x in (keys, values, segments, queries)),
-        scratch=[pltpu.VMEM((1, rows), jnp.int32), pltpu.SemaphoreType.DMA((2 + 4 * halves,))],
+        [buffer(kv_rows, HEAD)] * 2 + [buffer(rows, tiles * HEAD)] * 2,
+        [anywhere] * 5,
+        *(held(x) for x in (keys, values, segments, queries, stream)),
+        scratch=[pltpu.VMEM((1, rows), jnp.int32), pltpu.SemaphoreType.DMA((3 + 4 * halves,))],
     )
     packs = [
         keep,
@@ -279,21 +293,10 @@
         route(send, ["ctx"], lambda c: (up(other(c)),)),
     ]
     far_q = route(gate(far_q, packs[1]), ["ctx"], lambda c: (other(c),))
+    far_s = route(gate(far_s, packs[1]), ["ctx"], lambda c: (other(c),))
     for n in range(1, levels_back):
-        packs += [route(b, ["pipe", "ctx"], lambda p, c: hop(p, c, n)) for b in packs[-2:]]
-    (far,) = kernel(
-        functools.partial(stream_kernel, tiles),
-        "stream",
-        [buffer(rows, tiles * HEAD)],
-        [anywhere] * 3,
-        held(stream),
-        packs[2],
-        packs[3],
-        scratch=[pltpu.SemaphoreType.DMA((1,))],
-    )
-    far = route(far, ["ctx"], lambda c: (other(c),))
-
-    near, late = [0, 2, 3], [1, *range(4, len(packs))]
+        packs += [route(b, ["ctx", "tp"], lambda c, t: hop(c, t, n)) for b in packs[-2:]]
+    near, late = [0, 1, 2, 3], [*range(4, len(packs))]
     state = [jax.ShapeDtypeStruct((halves, group, rows, HEAD), jnp.float32)] * 3
     state = kernel(
         functools.partial(near_kernel, halves, group, near),
@@ -314,22 +317,22 @@
         *state,
         keep,
         *(packs[n] for n in late),
-        flops=1000000000,
+        flops=500000000,
     )
     straight = route(own, ["pipe"], lambda p: (after(p),))
     sq_a = route(own_sq, ["pipe", "tp"], lambda p, t: (after(p), 1 - t))
     (att,) = kernel(
-        functools.partial(part_kernel, halves, group),
+        functools.partial(part_kernel, halves, group, late),
         "attend_part",
         [buffer(rows, tiles * HEAD)],
         [vmem, anywhere] + [vmem] * len(packs),
         far_q,
         own,
         *packs,
-        flops=1000000000,
+        flops=500000000,
     )
     part, part_sq = kernel(
-        functools.partial(add_kernel, tiles), "add", [buffer(rows, tiles * HEAD), sums], [vmem] * 2, far, att
+        functools.partial(add_kernel, tiles), "add", [buffer(rows, tiles * HEAD), sums], [vmem] * 2, far_s, att
     )
     across = route(part, ["pipe", "ctx"], lambda p, c: (after(p), other(c)))
     sq_b = route(part_sq, ["pipe", "ctx", "tp"], lambda p, c, t: (after(p), other(c), 1 - t))

time: 35.6 us -> 34.3 us (0.963)
  Pallas kernels: 7.34 us -> 5.21 us
  starting transfers between devices: 15.8 us -> 16.4 us
    pallas_call x6 -> x5, Pallas kernels: 6.1 us -> 3.98 us  [kernel(): pl.pallas_call(body, out_shape=shapes, in_specs=specs, out_specs=[vmem] *...]
    ppermute x11, starting transfers between devices: 15.8 us -> 16.4 us  [route(): return lax.ppermute(x, tuple(axes) if len(axes) > 1 else axes[0], pairs)]
  transfers between devices with their start and end apart: 11 -> 11, of which waited for: 5 -> 5; matrix products, arithmetic and copies ran while one was open for 0% -> 0% of each run, Pallas kernels for 14% -> 8%
where the time goes in v4:
time: 34.3 us; the launch traced here: 33.8 us
  starting transfers between devices  16.4 us (48%)
  waiting for transfers between devices  11.5 us (34%)
  Pallas kernels  5.21 us (15%)
  between operations  0.7 us (2%)
    ppermute x11, starting transfers between devices, route(): return lax.ppermute(x, tuple(axes) if len(axes) > 1 else axes[0], pairs)  16.4 us
    ppermute x11, waiting for transfers between devices, route(): return lax.ppermute(x, tuple(axes) if len(axes) > 1 else axes[0], pairs)  11.5 us
    pallas_call x5, Pallas kernels, kernel(): pl.pallas_call(body, out_shape=shapes, in_specs=specs, out_specs=[vmem] *...  3.98 us
    pallas_call x1, Pallas kernels, per_device(): pl.pallas_call(functools.partial(final_kernel, tiles), out_shape=[buffer(...  1.23 us
  transfers between devices with their start and end apart: 11, of which 5 were waited for; matrix products, arithmetic and copies ran while one was open for 0% of the time, Pallas kernels for 8%

profile of v4, /device:TPU:1, one launch (start us, length us, event | category | flops | bytes accessed | tf_op | source)
XLA Modules:
  0.0 33.8 jit_solution(595672878693870417)
XLA Ops:
  0.6 1.3 %pack.1 = (bf16[528,128]{1,0:T(8,128)(2,1)S(1)}, bf16[528,128]{1,0:T(8,128)(2,1)S(1)}, bf16[128,1024]{1,0:T(8,128)(2,1)S(1)}, bf16[128,1024]{1,0:T(8,128)(2,1)S(1)}) custom-call(bf16[1,128,512]{2,1,0:T(8,128)(2,1)} %k_ref.1, bf16[1,128,512]{2,1,0:T(8,128)(2,1)} %v_ref.1, s32[1,128]{1,0:T(1,128)} %seg_ref.1, bf16[1,128,2048]{2,1,0:T(8,128)(2,1)} %q_ref.5, ...), custom_call_target="tpu_custom_call" | custom-call | tf_op jit(solution)/shard_map/pack/pallas_call | solution.py:269
  1.9 2.1 %collective-permute-start = (bf16[528,128]{1,0:T(8,128)(2,1)S(1)}, bf16[528,128]{1,0:T(8,128)(2,1)S(1)}, u32[]{:S(2)}, u32[]{:S(2)}) collective-permute-start(bf16[528,128]{1,0:T(8,128)(2,1)S(1)} %get-tuple-element.14), channel_id=1, source_target_pairs={{0,2},{2,0},{4,6},{6,4},{8,10},{10,8},{12,14},{14,12},{1,3},{3,1},... | collective-permute-start | bytes 405512 | tf_op jit(solution)/shard_map/ppermute | solution.py:33
  4.1 1.3 %collective-permute-start.1 = (bf16[528,128]{1,0:T(8,128)(2,1)S(1)}, bf16[528,128]{1,0:T(8,128)(2,1)S(1)}, u32[]{:S(2)}, u32[]{:S(2)}) collective-permute-start(bf16[528,128]{1,0:T(8,128)(2,1)S(1)} %get-tuple-element.13.refs_0_.keep), channel_id=1, source_target_pairs={{0,4},{2,6},{4,8},{6,10},{8,12},{10,14},{12,0},{14,2},{1,5},{3,7},... | collective-permute-start | bytes 405512 | tf_op jit(solution)/shard_map/ppermute | solution.py:33
  5.4 1.3 %collective-permute-start.2 = (bf16[528,128]{1,0:T(8,128)(2,1)S(1)}, bf16[528,128]{1,0:T(8,128)(2,1)S(1)}, u32[]{:S(2)}, u32[]{:S(2)}) collective-permute-start(bf16[528,128]{1,0:T(8,128)(2,1)S(1)} %get-tuple-element.14), channel_id=1, source_target_pairs={{0,6},{2,4},{4,10},{6,8},{8,14},{10,12},{12,2},{14,0},{1,7},{3,5},... | collective-permute-start | bytes 405512 | tf_op jit(solution)/shard_map/ppermute | solution.py:33
  6.6 0.7 %collective-permute-done.refs_1_ = bf16[528,128]{1,0:T(8,128)(2,1)S(1)} collective-permute-done((bf16[528,128]{1,0:T(8,128)(2,1)S(1)}, bf16[528,128]{1,0:T(8,128)(2,1)S(1)}, u32[]{:S(2)}, u32[]{:S(2)}) %collective-permute-start) | collective-permute-done | bytes 135200 | tf_op jit(solution)/shard_map/ppermute | solution.py:33
  7.4 1.1 %collective-permute-start.7 = (bf16[128,1024]{1,0:T(8,128)(2,1)S(1)}, bf16[128,1024]{1,0:T(8,128)(2,1)S(1)}, u32[]{:S(2)}, u32[]{:S(2)}) collective-permute-start(bf16[128,1024]{1,0:T(8,128)(2,1)S(1)} %gate.3), channel_id=1, source_target_pairs={{0,2},{2,0},{4,6},{6,4},{8,10},{10,8},{12,14},{14,12},{1,3},{3,1},... | collective-permute-start | bytes 786440 | tf_op jit(solution)/shard_map/ppermute | solution.py:33
  8.5 0.3 collective-permute-start.6
  8.8 1.3 %collective-permute-done.1.refs_2_ = bf16[528,128]{1,0:T(8,128)(2,1)S(1)} collective-permute-done((bf16[528,128]{1,0:T(8,128)(2,1)S(1)}, bf16[528,128]{1,0:T(8,128)(2,1)S(1)}, u32[]{:S(2)}, u32[]{:S(2)}) %collective-permute-start.1) | collective-permute-done | bytes 135200 | tf_op jit(solution)/shard_map/ppermute | solution.py:33
  10.1 3.2 %collective-permute-start.3 = (bf16[528,128]{1,0:T(8,128)(2,1)S(1)}, bf16[528,128]{1,0:T(8,128)(2,1)S(1)}, u32[]{:S(2)}, u32[]{:S(2)}) collective-permute-start(bf16[528,128]{1,0:T(8,128)(2,1)S(1)} %collective-permute-done.1.refs_2_), channel_id=1, source_target_pairs={{0,1},{1,0},{2,3},{3,2},{4,8},{5,9},{6,10},{7,11},{8,12},{9,13},{1... | collective-permute-start | bytes 405512 | tf_op jit(solution)/shard_map/ppermute | solution.py:33
  13.3 0.0 collective-permute-done.2.refs_3_
  13.4 1.5 %collective-permute-start.4 = (bf16[528,128]{1,0:T(8,128)(2,1)S(1)}, bf16[528,128]{1,0:T(8,128)(2,1)S(1)}, u32[]{:S(2)}, u32[]{:S(2)}) collective-permute-start(bf16[528,128]{1,0:T(8,128)(2,1)S(1)} %collective-permute-done.2.refs_3_), channel_id=1, source_target_pairs={{0,1},{1,0},{2,3},{3,2},{4,8},{5,9},{6,10},{7,11},{8,12},{9,13},{1... | collective-permute-start | bytes 405512 | tf_op jit(solution)/shard_map/ppermute | solution.py:33
  14.9 0.0 copy-done
  14.9 1.1 %attend_near.1 = (f32[2,4,128,128]{3,2,1,0:T(8,128)S(1)}, f32[2,4,128,128]{3,2,1,0:T(8,128)S(1)}, f32[2,4,128,128]{3,2,1,0:T(8,128)S(1)}) custom-call(bf16[1,128,2048]{2,1,0:T(8,128)(2,1)S(1)} %copy-done, bf16[528,128]{1,0:T(8,128)(2,1)S(1)} %get-tuple-element.13.refs_0_.keep, bf16[528,128]{1,0:T(8,128)(2,1)S(1)} %collective-permute-done.refs_1_, ...), custom_call_target="tpu_custom_call" | custom-call | flops 1000000000 | tf_op jit(solution)/shard_map/attend_near/pallas_call | solution.py:269
  16.0 0.0 collective-permute-done.3.refs_0_.refs_4_
  16.0 0.0 collective-permute-done.4.refs_1_.refs_5_
  16.0 0.0 copy-done.1
  16.0 0.3 attend_own.1
  16.3 1.3 %collective-permute-start.5 = (bf16[128,1024]{1,0:T(8,128)(2,1)S(1)}, bf16[128,1024]{1,0:T(8,128)(2,1)S(1)}, u32[]{:S(2)}, u32[]{:S(2)}) collective-permute-start(bf16[128,1024]{1,0:T(8,128)(2,1)S(1)} %get-tuple-element.18._), channel_id=1, source_target_pairs={{0,16},{16,0},{1,17},{17,1},{2,18},{18,2},{3,19},{19,3},{4,20},{20... | collective-permute-start | bytes 786440 | tf_op jit(solution)/shard_map/ppermute | solution.py:33
  17.6 0.0 collective-permute-done.7.q_ref
  17.6 1.1 %attend_part.1.att_ref = bf16[128,1024]{1,0:T(8,128)(2,1)S(1)} custom-call(bf16[128,1024]{1,0:T(8,128)(2,1)S(1)} %collective-permute-done.7.q_ref, bf16[128,1024]{1,0:T(8,128)(2,1)S(1)} %get-tuple-element.18._, bf16[528,128]{1,0:T(8,128)(2,1)S(1)} %get-tuple-element.13.refs_0_.keep, bf16[528,128]{1,0:T(8,128)(2,1)S(1)} %collective-permute-done.refs_1_, ...), custom_call_target="tpu_custom_call" | custom-call | flops 500000000 | tf_op jit(solution)/shard_map/attend_part/pallas_call | solution.py:269
  18.7 4.3 %collective-permute-done.6.s_ref = bf16[128,1024]{1,0:T(8,128)(2,1)S(1)} collective-permute-done((bf16[128,1024]{1,0:T(8,128)(2,1)S(1)}, bf16[128,1024]{1,0:T(8,128)(2,1)S(1)}, u32[]{:S(2)}, u32[]{:S(2)}) %collective-permute-start.6) | collective-permute-done | bytes 262176 | tf_op jit(solution)/shard_map/ppermute | solution.py:33
  23.0 0.2 add.1
  23.1 0.0 copy-start.2
  23.2 2.3 %collective-permute-start.8 = (bf16[128,1024]{1,0:T(8,128)(2,1)S(1)}, bf16[128,1024]{1,0:T(8,128)(2,1)S(1)}, u32[]{:S(2)}, u32[]{:S(2)}) collective-permute-start(bf16[128,1024]{1,0:T(8,128)(2,1)S(1)} %get-tuple-element.21), channel_id=1, source_target_pairs={{0,18},{2,16},{4,22},{6,20},{8,26},{10,24},{12,30},{14,28},{16,2},... | collective-permute-start | bytes 786440 | tf_op jit(solution)/shard_map/ppermute | solution.py:33
  25.5 1.9 %collective-permute-start.9 = (f32[8,128]{1,0:T(8,128)S(1)}, f32[8,128]{1,0:T(8,128)S(1)}, u32[]{:S(2)}, u32[]{:S(2)}) collective-permute-start(f32[8,128]{1,0:T(8,128)S(1)} %get-tuple-element.22), channel_id=1, source_target_pairs={{0,17},{1,16},{16,1},{17,0},{2,19},{3,18},{18,3},{19,2},{4,21},{5,... | collective-permute-start | bytes 12296 | tf_op jit(solution)/shard_map/ppermute | solution.py:33
  27.4 0.0 collective-permute-start.10
  27.4 0.0 copy-done.2
  27.4 1.9 %collective-permute-done.9.sq_a = f32[8,128]{1,0:T(8,128)S(1)} collective-permute-done((f32[8,128]{1,0:T(8,128)S(1)}, f32[8,128]{1,0:T(8,128)S(1)}, u32[]{:S(2)}, u32[]{:S(2)}) %collective-permute-start.9) | collective-permute-done | bytes 4128 | tf_op jit(solution)/shard_map/ppermute | solution.py:33
  29.3 3.2 %collective-permute-done.10.sq_b = f32[8,128]{1,0:T(8,128)S(1)} collective-permute-done((f32[8,128]{1,0:T(8,128)S(1)}, f32[8,128]{1,0:T(8,128)S(1)}, u32[]{:S(2)}, u32[]{:S(2)}) %collective-permute-start.10) | collective-permute-done | bytes 4128 | tf_op jit(solution)/shard_map/ppermute | solution.py:33
  32.5 0.0 collective-permute-done.5.own
  32.5 0.0 collective-permute-done.8.part
  32.5 1.2 %norm.1 = (bf16[1,128,2048]{2,1,0:T(8,128)(2,1)}, bf16[1,128,2048]{2,1,0:T(8,128)(2,1)}) custom-call(bf16[128,1024]{1,0:T(8,128)(2,1)S(1)} %collective-permute-done.5.own, bf16[128,1024]{1,0:T(8,128)(2,1)S(1)} %collective-permute-done.8.part, f32[8,128]{1,0:T(8,128)S(1)} %collective-permute-done.9.sq_a, f32[8,128]{1,0:T(8,128)S(1)} %collective-permute-done.10.sq_b, ...), custom_call_target="tpu_custom_call" | custom-call | tf_op jit(solution)/shard_map/norm/pallas_call | solution.py:340
  (5 shorter events, 0.0 us)
Async XLA Ops:
  1.9 5.4 %collective-permute-start = (bf16[528,128]{1,0:T(8,128)(2,1)S(1)}, bf16[528,128]{1,0:T(8,128)(2,1)S(1)}, u32[]{:S(2)}, u32[]{:S(2)}) collective-permute-start(bf16[528,128]{1,0:T(8,128)(2,1)S(1)} %get-tuple-element.14), channel_id=1, source_target_pairs={{0,2},{2,0},{4,6},{6,4},{8,10},{10,8},{12,14},{14,12},{1,3},{3,1},... | collective-permute-start | bytes 405512 | tf_op jit(solution)/shard_map/ppermute | solution.py:33
  4.1 6.1 %collective-permute-start.1 = (bf16[528,128]{1,0:T(8,128)(2,1)S(1)}, bf16[528,128]{1,0:T(8,128)(2,1)S(1)}, u32[]{:S(2)}, u32[]{:S(2)}) collective-permute-start(bf16[528,128]{1,0:T(8,128)(2,1)S(1)} %get-tuple-element.13.refs_0_.keep), channel_id=1, source_target_pairs={{0,4},{2,6},{4,8},{6,10},{8,12},{10,14},{12,0},{14,2},{1,5},{3,7},... | collective-permute-start | bytes 405512 | tf_op jit(solution)/shard_map/ppermute | solution.py:33
  5.4 8.0 %collective-permute-start.2 = (bf16[528,128]{1,0:T(8,128)(2,1)S(1)}, bf16[528,128]{1,0:T(8,128)(2,1)S(1)}, u32[]{:S(2)}, u32[]{:S(2)}) collective-permute-start(bf16[528,128]{1,0:T(8,128)(2,1)S(1)} %get-tuple-element.14), channel_id=1, source_target_pairs={{0,6},{2,4},{4,10},{6,8},{8,14},{10,12},{12,2},{14,0},{1,7},{3,5},... | collective-permute-start | bytes 405512 | tf_op jit(solution)/shard_map/ppermute | solution.py:33
  7.4 7.5 %copy-start = (bf16[1,128,2048]{2,1,0:T(8,128)(2,1)S(1)}, bf16[1,128,2048]{2,1,0:T(8,128)(2,1)}, u32[]{:S(2)}) copy-start(bf16[1,128,2048]{2,1,0:T(8,128)(2,1)} %q_ref.5) | copy-start | bytes 1572868
  7.4 10.2 %collective-permute-start.7 = (bf16[128,1024]{1,0:T(8,128)(2,1)S(1)}, bf16[128,1024]{1,0:T(8,128)(2,1)S(1)}, u32[]{:S(2)}, u32[]{:S(2)}) collective-permute-start(bf16[128,1024]{1,0:T(8,128)(2,1)S(1)} %gate.3), channel_id=1, source_target_pairs={{0,2},{2,0},{4,6},{6,4},{8,10},{10,8},{12,14},{14,12},{1,3},{3,1},... | collective-permute-start | bytes 786440 | tf_op jit(solution)/shard_map/ppermute | solution.py:33
  8.5 7.5 %copy-start.1 = (bf16[1,128,2048]{2,1,0:T(8,128)(2,1)S(1)}, bf16[1,128,2048]{2,1,0:T(8,128)(2,1)}, u32[]{:S(2)}) copy-start(bf16[1,128,2048]{2,1,0:T(8,128)(2,1)} %s_ref.3) | copy-start | bytes 1572868
  8.5 14.4 %collective-permute-start.6 = (bf16[128,1024]{1,0:T(8,128)(2,1)S(1)}, bf16[128,1024]{1,0:T(8,128)(2,1)S(1)}, u32[]{:S(2)}, u32[]{:S(2)}) collective-permute-start(bf16[128,1024]{1,0:T(8,128)(2,1)S(1)} %gate.2), channel_id=1, source_target_pairs={{0,2},{2,0},{4,6},{6,4},{8,10},{10,8},{12,14},{14,12},{1,3},{3,1},... | collective-permute-start | bytes 786440 | tf_op jit(solution)/shard_map/ppermute | solution.py:33
  10.1 5.9 %collective-permute-start.3 = (bf16[528,128]{1,0:T(8,128)(2,1)S(1)}, bf16[528,128]{1,0:T(8,128)(2,1)S(1)}, u32[]{:S(2)}, u32[]{:S(2)}) collective-permute-start(bf16[528,128]{1,0:T(8,128)(2,1)S(1)} %collective-permute-done.1.refs_2_), channel_id=1, source_target_pairs={{0,1},{1,0},{2,3},{3,2},{4,8},{5,9},{6,10},{7,11},{8,12},{9,13},{1... | collective-permute-start | bytes 405512 | tf_op jit(solution)/shard_map/ppermute | solution.py:33
  13.4 2.7 %collective-permute-start.4 = (bf16[528,128]{1,0:T(8,128)(2,1)S(1)}, bf16[528,128]{1,0:T(8,128)(2,1)S(1)}, u32[]{:S(2)}, u32[]{:S(2)}) collective-permute-start(bf16[528,128]{1,0:T(8,128)(2,1)S(1)} %collective-permute-done.2.refs_3_), channel_id=1, source_target_pairs={{0,1},{1,0},{2,3},{3,2},{4,8},{5,9},{6,10},{7,11},{8,12},{9,13},{1... | collective-permute-start | bytes 405512 | tf_op jit(solution)/shard_map/ppermute | solution.py:33
  16.3 16.2 %collective-permute-start.5 = (bf16[128,1024]{1,0:T(8,128)(2,1)S(1)}, bf16[128,1024]{1,0:T(8,128)(2,1)S(1)}, u32[]{:S(2)}, u32[]{:S(2)}) collective-permute-start(bf16[128,1024]{1,0:T(8,128)(2,1)S(1)} %get-tuple-element.18._), channel_id=1, source_target_pairs={{0,16},{16,0},{1,17},{17,1},{2,18},{18,2},{3,19},{19,3},{4,20},{20... | collective-permute-start | bytes 786440 | tf_op jit(solution)/shard_map/ppermute | solution.py:33
  23.1 4.3 %copy-start.2 = (bf16[2048]{0:T(1024)(128)(2,1)S(1)}, bf16[2048]{0:T(1024)(128)(2,1)}, u32[]{:S(2)}) copy-start(bf16[2048]{0:T(1024)(128)(2,1)} %param.11) | copy-start | bytes 12292
  23.2 9.4 %collective-permute-start.8 = (bf16[128,1024]{1,0:T(8,128)(2,1)S(1)}, bf16[128,1024]{1,0:T(8,128)(2,1)S(1)}, u32[]{:S(2)}, u32[]{:S(2)}) collective-permute-start(bf16[128,1024]{1,0:T(8,128)(2,1)S(1)} %get-tuple-element.21), channel_id=1, source_target_pairs={{0,18},{2,16},{4,22},{6,20},{8,26},{10,24},{12,30},{14,28},{16,2},... | collective-permute-start | bytes 786440 | tf_op jit(solution)/shard_map/ppermute | solution.py:33
  25.5 3.9 %collective-permute-start.9 = (f32[8,128]{1,0:T(8,128)S(1)}, f32[8,128]{1,0:T(8,128)S(1)}, u32[]{:S(2)}, u32[]{:S(2)}) collective-permute-start(f32[8,128]{1,0:T(8,128)S(1)} %get-tuple-element.22), channel_id=1, source_target_pairs={{0,17},{1,16},{16,1},{17,0},{2,19},{3,18},{18,3},{19,2},{4,21},{5,... | collective-permute-start | bytes 12296 | tf_op jit(solution)/shard_map/ppermute | solution.py:33
  27.4 5.2 %collective-permute-start.10 = (f32[8,128]{1,0:T(8,128)S(1)}, f32[8,128]{1,0:T(8,128)S(1)}, u32[]{:S(2)}, u32[]{:S(2)}) collective-permute-start(f32[8,128]{1,0:T(8,128)S(1)} %get-tuple-element.23), channel_id=1, source_target_pairs={{0,19},{1,18},{2,17},{3,16},{4,23},{5,22},{6,21},{7,20},{8,27},{9,... | collective-permute-start | bytes 12296 | tf_op jit(solution)/shard_map/ppermute | solution.py:33

commit v5 on v4

--- a/solution.py
+++ b/solution.py
@@ -66,9 +66,8 @@
     return pl.ds(pl.multiple_of(start * HEAD, HEAD), size * HEAD)
 
 
-def pack_kernel(halves, group, k_ref, v_ref, seg_ref, q_ref, s_ref, keep, send, far_q, far_s, seg_buf, sems):
-    side = lax.axis_index("ctx") % 2
-    tiles = halves * group
+def pack_kernel(halves, k_ref, v_ref, seg_ref, keep, send, seg_buf, sems):
+    side = lax.axis_index("ctx") % 2
     fetches = Fetches(sems)
     fetches.start(seg_ref, seg_buf)
     for out, half in ((keep, side), (send, 1 - side)):
@@ -76,12 +75,18 @@
             for n, ref in enumerate((k_ref, v_ref)):
                 rows = pl.ds((2 * h + n) * HEAD, HEAD)
                 fetches.start(ref.at[0, :, lanes(half * halves + h, 1)], out.at[rows])
-    for ref, far in ((q_ref, far_q), (s_ref, far_s)):
-        fetches.start(ref.at[0, :, lanes((1 - side) * tiles, tiles)], far)
     fetches.wait()
     seg = jnp.broadcast_to(seg_buf[...], (SEG_ROWS, HEAD)).astype(jnp.float32).astype(jnp.bfloat16)
     for out in (keep, send):
         out[2 * halves * HEAD :, :] = seg
+
+
+def rows_kernel(tiles, q_ref, s_ref, _, far_q, far_s, sems):
+    side = lax.axis_index("ctx") % 2
+    fetches = Fetches(sems)
+    for ref, far in ((q_ref, far_q), (s_ref, far_s)):
+        fetches.start(ref.at[0, :, lanes((1 - side) * tiles, tiles)], far)
+    fetches.wait()
 
 
 def masks(halves, own, packs, blocks):
@@ -278,13 +283,13 @@
         )(*args)
 
     kv_rows = 2 * halves * HEAD + SEG_ROWS
-    keep, send, far_q, far_s = kernel(
-        functools.partial(pack_kernel, halves, group),
+    keep, send = kernel(
+        functools.partial(pack_kernel, halves),
         "pack",
-        [buffer(kv_rows, HEAD)] * 2 + [buffer(rows, tiles * HEAD)] * 2,
-        [anywhere] * 5,
-        *(held(x) for x in (keys, values, segments, queries, stream)),
-        scratch=[pltpu.VMEM((1, rows), jnp.int32), pltpu.SemaphoreType.DMA((3 + 4 * halves,))],
+        [buffer(kv_rows, HEAD)] * 2,
+        [anywhere] * 3,
+        *(held(x) for x in (keys, values, segments)),
+        scratch=[pltpu.VMEM((1, rows), jnp.int32), pltpu.SemaphoreType.DMA((1 + 4 * halves,))],
     )
     packs = [
         keep,
@@ -292,6 +297,17 @@
         route(keep, ["ctx"], lambda c: (up(c),)),
         route(send, ["ctx"], lambda c: (up(other(c)),)),
     ]
+    far_q, far_s = kernel(
+        functools.partial(rows_kernel, tiles),
+        "rows",
+        [buffer(rows, tiles * HEAD)] * 2,
+        [anywhere] * 3,
+        held(queries),
+        held(stream),
+        keep,
+        scratch=[pltpu.SemaphoreType.DMA((2,))],
+        flops=2000000000,
+    )
     far_q = route(gate(far_q, packs[1]), ["ctx"], lambda c: (other(c),))
     far_s = route(gate(far_s, packs[1]), ["ctx"], lambda c: (other(c),))
     for n in range(1, levels_back):

time: 34.3 us -> 33.8 us (0.985)
  starting transfers between devices: 16.4 us -> 13 us
  waiting for transfers between devices: 11.5 us -> 13.6 us
  Pallas kernels: 5.21 us -> 5.88 us
    ppermute x11, starting transfers between devices: 16.4 us -> 13 us  [route(): return lax.ppermute(x, tuple(axes) if len(axes) > 1 else axes[0], pairs)]
    ppermute x11, waiting for transfers between devices: 11.5 us -> 13.6 us  [route(): return lax.ppermute(x, tuple(axes) if len(axes) > 1 else axes[0], pairs)]
    pallas_call x5 -> x6, Pallas kernels: 3.98 us -> 4.65 us  [kernel(): pl.pallas_call(body, out_shape=shapes, in_specs=specs, out_specs=[vmem] *...]
  transfers between devices with their start and end apart: 11 -> 11, of which waited for: 5 -> 5; matrix products, arithmetic and copies ran while one was open for 0% -> 0% of each run, Pallas kernels for 8% -> 11%
where the time goes in v5:
time: 33.8 us; the launch traced here: 33.2 us
  waiting for transfers between devices  13.6 us (40%)
  starting transfers between devices  13 us (38%)
  Pallas kernels  5.88 us (17%)
  between operations  0.72 us (2%)
    ppermute x11, waiting for transfers between devices, route(): return lax.ppermute(x, tuple(axes) if len(axes) > 1 else axes[0], pairs)  13.6 us
    ppermute x11, starting transfers between devices, route(): return lax.ppermute(x, tuple(axes) if len(axes) > 1 else axes[0], pairs)  13 us
    pallas_call x6, Pallas kernels, kernel(): pl.pallas_call(body, out_shape=shapes, in_specs=specs, out_specs=[vmem] *...  4.65 us
    pallas_call x1, Pallas kernels, per_device(): pl.pallas_call(functools.partial(final_kernel, tiles), out_shape=[buffer(...  1.23 us
  transfers between devices with their start and end apart: 11, of which 5 were waited for; matrix products, arithmetic and copies ran while one was open for 0% of the time, Pallas kernels for 11%

profile of v5, /device:TPU:1, one launch (start us, length us, event | category | flops | bytes accessed | tf_op | source)
XLA Modules:
  0.0 33.2 jit_solution(9754891259808546765)
XLA Ops:
  0.6 1.0 %pack.1 = (bf16[528,128]{1,0:T(8,128)(2,1)S(1)}, bf16[528,128]{1,0:T(8,128)(2,1)S(1)}) custom-call(bf16[1,128,512]{2,1,0:T(8,128)(2,1)} %k_ref.1, bf16[1,128,512]{2,1,0:T(8,128)(2,1)} %v_ref.1, s32[1,128]{1,0:T(1,128)} %seg_ref.1), custom_call_target="tpu_custom_call" | custom-call | tf_op jit(solution)/shard_map/pack/pallas_call | solution.py:274
  1.6 2.1 %collective-permute-start = (bf16[528,128]{1,0:T(8,128)(2,1)S(1)}, bf16[528,128]{1,0:T(8,128)(2,1)S(1)}, u32[]{:S(2)}, u32[]{:S(2)}) collective-permute-start(bf16[528,128]{1,0:T(8,128)(2,1)S(1)} %get-tuple-element.14), channel_id=1, source_target_pairs={{0,2},{2,0},{4,6},{6,4},{8,10},{10,8},{12,14},{14,12},{1,3},{3,1},... | collective-permute-start | bytes 405512 | tf_op jit(solution)/shard_map/ppermute | solution.py:33
  3.7 1.3 %collective-permute-start.2 = (bf16[528,128]{1,0:T(8,128)(2,1)S(1)}, bf16[528,128]{1,0:T(8,128)(2,1)S(1)}, u32[]{:S(2)}, u32[]{:S(2)}) collective-permute-start(bf16[528,128]{1,0:T(8,128)(2,1)S(1)} %get-tuple-element.14), channel_id=1, source_target_pairs={{0,6},{2,4},{4,10},{6,8},{8,14},{10,12},{12,2},{14,0},{1,7},{3,5},... | collective-permute-start | bytes 405512 | tf_op jit(solution)/shard_map/ppermute | solution.py:33
  5.0 1.3 %collective-permute-start.1 = (bf16[528,128]{1,0:T(8,128)(2,1)S(1)}, bf16[528,128]{1,0:T(8,128)(2,1)S(1)}, u32[]{:S(2)}, u32[]{:S(2)}) collective-permute-start(bf16[528,128]{1,0:T(8,128)(2,1)S(1)} %get-tuple-element.13.refs_0_.keep._), channel_id=1, source_target_pairs={{0,4},{2,6},{4,8},{6,10},{8,12},{10,14},{12,0},{14,2},{1,5},{3,7},... | collective-permute-start | bytes 405512 | tf_op jit(solution)/shard_map/ppermute | solution.py:33
  6.3 1.0 %rows.1 = (bf16[128,1024]{1,0:T(8,128)(2,1)S(1)}, bf16[128,1024]{1,0:T(8,128)(2,1)S(1)}) custom-call(bf16[1,128,2048]{2,1,0:T(8,128)(2,1)} %q_ref.5, bf16[1,128,2048]{2,1,0:T(8,128)(2,1)} %s_ref.3, bf16[528,128]{1,0:T(8,128)(2,1)S(1)} %get-tuple-element.13.refs_0_.keep._), custom_call_target="tpu_custom_call" | custom-call | flops 2000000000 | tf_op jit(solution)/shard_map/rows/pallas_call | solution.py:274
  7.3 0.0 collective-permute-done.refs_1_
  7.3 0.0 copy-start
  7.4 1.3 %collective-permute-start.7 = (bf16[128,1024]{1,0:T(8,128)(2,1)S(1)}, bf16[128,1024]{1,0:T(8,128)(2,1)S(1)}, u32[]{:S(2)}, u32[]{:S(2)}) collective-permute-start(bf16[128,1024]{1,0:T(8,128)(2,1)S(1)} %gate.3), channel_id=1, source_target_pairs={{0,2},{2,0},{4,6},{6,4},{8,10},{10,8},{12,14},{14,12},{1,3},{3,1},... | collective-permute-start | bytes 786440 | tf_op jit(solution)/shard_map/ppermute | solution.py:33
  8.6 0.3 collective-permute-start.6
  8.9 4.0 %collective-permute-done.1.refs_2_ = bf16[528,128]{1,0:T(8,128)(2,1)S(1)} collective-permute-done((bf16[528,128]{1,0:T(8,128)(2,1)S(1)}, bf16[528,128]{1,0:T(8,128)(2,1)S(1)}, u32[]{:S(2)}, u32[]{:S(2)}) %collective-permute-start.1) | collective-permute-done | bytes 135200 | tf_op jit(solution)/shard_map/ppermute | solution.py:33
  12.9 1.5 %collective-permute-start.3 = (bf16[528,128]{1,0:T(8,128)(2,1)S(1)}, bf16[528,128]{1,0:T(8,128)(2,1)S(1)}, u32[]{:S(2)}, u32[]{:S(2)}) collective-permute-start(bf16[528,128]{1,0:T(8,128)(2,1)S(1)} %collective-permute-done.1.refs_2_), channel_id=1, source_target_pairs={{0,1},{1,0},{2,3},{3,2},{4,8},{5,9},{6,10},{7,11},{8,12},{9,13},{1... | collective-permute-start | bytes 405512 | tf_op jit(solution)/shard_map/ppermute | solution.py:33
  14.5 0.0 collective-permute-done.2.refs_3_
  14.5 0.0 collective-permute-start.4
  14.5 0.0 copy-done
  14.5 1.1 %attend_near.1 = (f32[2,4,128,128]{3,2,1,0:T(8,128)S(1)}, f32[2,4,128,128]{3,2,1,0:T(8,128)S(1)}, f32[2,4,128,128]{3,2,1,0:T(8,128)S(1)}) custom-call(bf16[1,128,2048]{2,1,0:T(8,128)(2,1)S(1)} %copy-done, bf16[528,128]{1,0:T(8,128)(2,1)S(1)} %get-tuple-element.13.refs_0_.keep._, bf16[528,128]{1,0:T(8,128)(2,1)S(1)} %collective-permute-done.refs_1_, ...), custom_call_target="tpu_custom_call" | custom-call | flops 1000000000 | tf_op jit(solution)/shard_map/attend_near/pallas_call | solution.py:274
  15.6 0.0 collective-permute-done.3.refs_0_.refs_4_
  15.6 0.2 collective-permute-done.4.refs_1_.refs_5_
  15.8 0.3 attend_own.1
  16.1 1.3 %collective-permute-start.5 = (bf16[128,1024]{1,0:T(8,128)(2,1)S(1)}, bf16[128,1024]{1,0:T(8,128)(2,1)S(1)}, u32[]{:S(2)}, u32[]{:S(2)}) collective-permute-start(bf16[128,1024]{1,0:T(8,128)(2,1)S(1)} %get-tuple-element.18._), channel_id=1, source_target_pairs={{0,16},{16,0},{1,17},{17,1},{2,18},{18,2},{3,19},{19,3},{4,20},{20... | collective-permute-start | bytes 786440 | tf_op jit(solution)/shard_map/ppermute | solution.py:33
  17.4 0.0 collective-permute-done.7.q_ref
  17.4 1.1 %attend_part.1.att_ref = bf16[128,1024]{1,0:T(8,128)(2,1)S(1)} custom-call(bf16[128,1024]{1,0:T(8,128)(2,1)S(1)} %collective-permute-done.7.q_ref, bf16[128,1024]{1,0:T(8,128)(2,1)S(1)} %get-tuple-element.18._, bf16[528,128]{1,0:T(8,128)(2,1)S(1)} %get-tuple-element.13.refs_0_.keep._, bf16[528,128]{1,0:T(8,128)(2,1)S(1)} %collective-permute-done.refs_1_, ...), custom_call_target="tpu_custom_call" | custom-call | flops 500000000 | tf_op jit(solution)/shard_map/attend_part/pallas_call | solution.py:274
  18.5 3.9 %collective-permute-done.6.s_ref = bf16[128,1024]{1,0:T(8,128)(2,1)S(1)} collective-permute-done((bf16[128,1024]{1,0:T(8,128)(2,1)S(1)}, bf16[128,1024]{1,0:T(8,128)(2,1)S(1)}, u32[]{:S(2)}, u32[]{:S(2)}) %collective-permute-start.6) | collective-permute-done | bytes 262176 | tf_op jit(solution)/shard_map/ppermute | solution.py:33
  22.4 0.2 add.1
  22.6 0.0 copy-start.2
  22.6 1.3 %collective-permute-start.8 = (bf16[128,1024]{1,0:T(8,128)(2,1)S(1)}, bf16[128,1024]{1,0:T(8,128)(2,1)S(1)}, u32[]{:S(2)}, u32[]{:S(2)}) collective-permute-start(bf16[128,1024]{1,0:T(8,128)(2,1)S(1)} %get-tuple-element.21), channel_id=1, source_target_pairs={{0,18},{2,16},{4,22},{6,20},{8,26},{10,24},{12,30},{14,28},{16,2},... | collective-permute-start | bytes 786440 | tf_op jit(solution)/shard_map/ppermute | solution.py:33
  23.9 1.7 %collective-permute-start.9 = (f32[8,128]{1,0:T(8,128)S(1)}, f32[8,128]{1,0:T(8,128)S(1)}, u32[]{:S(2)}, u32[]{:S(2)}) collective-permute-start(f32[8,128]{1,0:T(8,128)S(1)} %get-tuple-element.22), channel_id=1, source_target_pairs={{0,17},{1,16},{16,1},{17,0},{2,19},{3,18},{18,3},{19,2},{4,21},{5,... | collective-permute-start | bytes 12296 | tf_op jit(solution)/shard_map/ppermute | solution.py:33
  25.7 0.9 %collective-permute-start.10 = (f32[8,128]{1,0:T(8,128)S(1)}, f32[8,128]{1,0:T(8,128)S(1)}, u32[]{:S(2)}, u32[]{:S(2)}) collective-permute-start(f32[8,128]{1,0:T(8,128)S(1)} %get-tuple-element.23), channel_id=1, source_target_pairs={{0,19},{1,18},{2,17},{3,16},{4,23},{5,22},{6,21},{7,20},{8,27},{9,... | collective-permute-start | bytes 12296 | tf_op jit(solution)/shard_map/ppermute | solution.py:33
  26.6 0.8 %collective-permute-done.9.sq_a = f32[8,128]{1,0:T(8,128)S(1)} collective-permute-done((f32[8,128]{1,0:T(8,128)S(1)}, f32[8,128]{1,0:T(8,128)S(1)}, u32[]{:S(2)}, u32[]{:S(2)}) %collective-permute-start.9) | collective-permute-done | bytes 4128 | tf_op jit(solution)/shard_map/ppermute | solution.py:33
  27.4 4.6 %collective-permute-done.10.sq_b = f32[8,128]{1,0:T(8,128)S(1)} collective-permute-done((f32[8,128]{1,0:T(8,128)S(1)}, f32[8,128]{1,0:T(8,128)S(1)}, u32[]{:S(2)}, u32[]{:S(2)}) %collective-permute-start.10) | collective-permute-done | bytes 4128 | tf_op jit(solution)/shard_map/ppermute | solution.py:33
  32.0 0.0 collective-permute-done.5.own
  32.0 0.0 collective-permute-done.8.part
  32.0 1.2 %norm.1 = (bf16[1,128,2048]{2,1,0:T(8,128)(2,1)}, bf16[1,128,2048]{2,1,0:T(8,128)(2,1)}) custom-call(bf16[128,1024]{1,0:T(8,128)(2,1)S(1)} %collective-permute-done.5.own, bf16[128,1024]{1,0:T(8,128)(2,1)S(1)} %collective-permute-done.8.part, f32[8,128]{1,0:T(8,128)S(1)} %collective-permute-done.9.sq_a, f32[8,128]{1,0:T(8,128)S(1)} %collective-permute-done.10.sq_b, ...), custom_call_target="tpu_custom_call" | custom-call | tf_op jit(solution)/shard_map/norm/pallas_call | solution.py:356
  (6 shorter events, 0.0 us)
Async XLA Ops:
  1.6 5.7 %collective-permute-start = (bf16[528,128]{1,0:T(8,128)(2,1)S(1)}, bf16[528,128]{1,0:T(8,128)(2,1)S(1)}, u32[]{:S(2)}, u32[]{:S(2)}) collective-permute-start(bf16[528,128]{1,0:T(8,128)(2,1)S(1)} %get-tuple-element.14), channel_id=1, source_target_pairs={{0,2},{2,0},{4,6},{6,4},{8,10},{10,8},{12,14},{14,12},{1,3},{3,1},... | collective-permute-start | bytes 405512 | tf_op jit(solution)/shard_map/ppermute | solution.py:33
  3.7 10.8 %collective-permute-start.2 = (bf16[528,128]{1,0:T(8,128)(2,1)S(1)}, bf16[528,128]{1,0:T(8,128)(2,1)S(1)}, u32[]{:S(2)}, u32[]{:S(2)}) collective-permute-start(bf16[528,128]{1,0:T(8,128)(2,1)S(1)} %get-tuple-element.14), channel_id=1, source_target_pairs={{0,6},{2,4},{4,10},{6,8},{8,14},{10,12},{12,2},{14,0},{1,7},{3,5},... | collective-permute-start | bytes 405512 | tf_op jit(solution)/shard_map/ppermute | solution.py:33
  5.0 7.9 %collective-permute-start.1 = (bf16[528,128]{1,0:T(8,128)(2,1)S(1)}, bf16[528,128]{1,0:T(8,128)(2,1)S(1)}, u32[]{:S(2)}, u32[]{:S(2)}) collective-permute-start(bf16[528,128]{1,0:T(8,128)(2,1)S(1)} %get-tuple-element.13.refs_0_.keep._), channel_id=1, source_target_pairs={{0,4},{2,6},{4,8},{6,10},{8,12},{10,14},{12,0},{14,2},{1,5},{3,7},... | collective-permute-start | bytes 405512 | tf_op jit(solution)/shard_map/ppermute | solution.py:33
  7.3 7.1 %copy-start = (bf16[1,128,2048]{2,1,0:T(8,128)(2,1)S(1)}, bf16[1,128,2048]{2,1,0:T(8,128)(2,1)}, u32[]{:S(2)}) copy-start(bf16[1,128,2048]{2,1,0:T(8,128)(2,1)} %q_ref.5) | copy-start | bytes 1572868
  7.4 10.0 %collective-permute-start.7 = (bf16[128,1024]{1,0:T(8,128)(2,1)S(1)}, bf16[128,1024]{1,0:T(8,128)(2,1)S(1)}, u32[]{:S(2)}, u32[]{:S(2)}) collective-permute-start(bf16[128,1024]{1,0:T(8,128)(2,1)S(1)} %gate.3), channel_id=1, source_target_pairs={{0,2},{2,0},{4,6},{6,4},{8,10},{10,8},{12,14},{14,12},{1,3},{3,1},... | collective-permute-start | bytes 786440 | tf_op jit(solution)/shard_map/ppermute | solution.py:33
  8.6 7.2 %copy-start.1 = (bf16[1,128,2048]{2,1,0:T(8,128)(2,1)S(1)}, bf16[1,128,2048]{2,1,0:T(8,128)(2,1)}, u32[]{:S(2)}) copy-start(bf16[1,128,2048]{2,1,0:T(8,128)(2,1)} %s_ref.3) | copy-start | bytes 1572868
  8.6 13.8 %collective-permute-start.6 = (bf16[128,1024]{1,0:T(8,128)(2,1)S(1)}, bf16[128,1024]{1,0:T(8,128)(2,1)S(1)}, u32[]{:S(2)}, u32[]{:S(2)}) collective-permute-start(bf16[128,1024]{1,0:T(8,128)(2,1)S(1)} %gate.2), channel_id=1, source_target_pairs={{0,2},{2,0},{4,6},{6,4},{8,10},{10,8},{12,14},{14,12},{1,3},{3,1},... | collective-permute-start | bytes 786440 | tf_op jit(solution)/shard_map/ppermute | solution.py:33
  12.9 2.7 %collective-permute-start.3 = (bf16[528,128]{1,0:T(8,128)(2,1)S(1)}, bf16[528,128]{1,0:T(8,128)(2,1)S(1)}, u32[]{:S(2)}, u32[]{:S(2)}) collective-permute-start(bf16[528,128]{1,0:T(8,128)(2,1)S(1)} %collective-permute-done.1.refs_2_), channel_id=1, source_target_pairs={{0,1},{1,0},{2,3},{3,2},{4,8},{5,9},{6,10},{7,11},{8,12},{9,13},{1... | collective-permute-start | bytes 405512 | tf_op jit(solution)/shard_map/ppermute | solution.py:33
  14.5 1.4 %collective-permute-start.4 = (bf16[528,128]{1,0:T(8,128)(2,1)S(1)}, bf16[528,128]{1,0:T(8,128)(2,1)S(1)}, u32[]{:S(2)}, u32[]{:S(2)}) collective-permute-start(bf16[528,128]{1,0:T(8,128)(2,1)S(1)} %collective-permute-done.2.refs_3_), channel_id=1, source_target_pairs={{0,1},{1,0},{2,3},{3,2},{4,8},{5,9},{6,10},{7,11},{8,12},{9,13},{1... | collective-permute-start | bytes 405512 | tf_op jit(solution)/shard_map/ppermute | solution.py:33
  16.1 15.9 %collective-permute-start.5 = (bf16[128,1024]{1,0:T(8,128)(2,1)S(1)}, bf16[128,1024]{1,0:T(8,128)(2,1)S(1)}, u32[]{:S(2)}, u32[]{:S(2)}) collective-permute-start(bf16[128,1024]{1,0:T(8,128)(2,1)S(1)} %get-tuple-element.18._), channel_id=1, source_target_pairs={{0,16},{16,0},{1,17},{17,1},{2,18},{18,2},{3,19},{19,3},{4,20},{20... | collective-permute-start | bytes 786440 | tf_op jit(solution)/shard_map/ppermute | solution.py:33
  22.6 4.0 %copy-start.2 = (bf16[2048]{0:T(1024)(128)(2,1)S(1)}, bf16[2048]{0:T(1024)(128)(2,1)}, u32[]{:S(2)}) copy-start(bf16[2048]{0:T(1024)(128)(2,1)} %param.11) | copy-start | bytes 12292
  22.6 9.4 %collective-permute-start.8 = (bf16[128,1024]{1,0:T(8,128)(2,1)S(1)}, bf16[128,1024]{1,0:T(8,128)(2,1)S(1)}, u32[]{:S(2)}, u32[]{:S(2)}) collective-permute-start(bf16[128,1024]{1,0:T(8,128)(2,1)S(1)} %get-tuple-element.21), channel_id=1, source_target_pairs={{0,18},{2,16},{4,22},{6,20},{8,26},{10,24},{12,30},{14,28},{16,2},... | collective-permute-start | bytes 786440 | tf_op jit(solution)/shard_map/ppermute | solution.py:33
  23.9 3.4 %collective-permute-start.9 = (f32[8,128]{1,0:T(8,128)S(1)}, f32[8,128]{1,0:T(8,128)S(1)}, u32[]{:S(2)}, u32[]{:S(2)}) collective-permute-start(f32[8,128]{1,0:T(8,128)S(1)} %get-tuple-element.22), channel_id=1, source_target_pairs={{0,17},{1,16},{16,1},{17,0},{2,19},{3,18},{18,3},{19,2},{4,21},{5,... | collective-permute-start | bytes 12296 | tf_op jit(solution)/shard_map/ppermute | solution.py:33
  25.7 6.3 %collective-permute-start.10 = (f32[8,128]{1,0:T(8,128)S(1)}, f32[8,128]{1,0:T(8,128)S(1)}, u32[]{:S(2)}, u32[]{:S(2)}) collective-permute-start(f32[8,128]{1,0:T(8,128)S(1)} %get-tuple-element.23), channel_id=1, source_target_pairs={{0,19},{1,18},{2,17},{3,16},{4,23},{5,22},{6,21},{7,20},{8,27},{9,... | collective-permute-start | bytes 12296 | tf_op jit(solution)/shard_map/ppermute | solution.py:33
